TPU v7x, 256 devices: a whole 4x4x8 slice. The times are simulated.
256 devices in a mesh: band: 4 (over y_lo, core), pw: 64 (over z, y_hi, x).
Axes of the slice: x: 4, y: 4 (y_hi: 2, y_lo: 2; y = y_hi * 2 + y_lo), z: 8, core: 2. Of those that a mesh axis runs over, the one named last changes fastest.
Arguments:
- orbitals: bfloat16 [4, 2, 192, 16384], P('band', None, None, 'pw'), may hold values from -6 to 6
- column_map: int32 [16384], replicated, may hold values from 0 to 36863, as said below
- potential: float32 [192, 192, 192], P('pw'), may hold values from -1.5 to 1
- projectors: bfloat16 [32768, 8, 128], P('pw'), may hold values from -0.59765625 to 0.59765625
- block_index: int32 [32768], P('pw'), may hold values from 0 to 863, as said below
- block_atom: int32 [32768], P('pw'), may hold values from 0 to 1999, as said below
- coupling: float32 [2000, 8, 8], replicated, may hold values from -1.2 to 1.2
Outputs:
- applied: float32 [4, 2, 192, 16384], P('band', None, None, 'pw')
- subspace: float32 [2, 4, 4], P(None, None, 'band')
Inputs may be any that keep to these rules, and one draw needn't show every extreme that they name: `column_map`: distinct grid columns, each numbered x * 192 + y; they are the 16384 columns nearest signed frequency (0, 0), that is with the smallest fx*fx + fy*fy, ties in any order. `block_index`: A block of the planes of the device that holds the entry. `block_atom`: with n the length of the pw axis and r = floor(2000 / n), an entry on pw device p names an atom a with (a - floor(p * 2000 / n) + 2 r) mod 2000 at most 5 r. Several entries may name one atom, and one block.
All inputs are finite; a program needn't handle non-finite values.
Results may differ from a plain program's by a relative error of at most 0.00031.
The roundings to bfloat16 on the way count: a program that leaves them out, or rounds other values in their place, can miss the bound.
Values may be sent and summed in bfloat16 or wider, within the bound.
No kernel may reach another device: no remote copies, remote signals or barrier semaphores. Data moves between devices by JAX's collectives and lax.ppermute only.
A program may use at most 128 MiB of HBM per device.

v0:
```python
import math

import jax
import jax.numpy as jnp
import numpy as np
from jax import lax
from jax.experimental import pallas as pl
from jax.experimental.pallas import tpu as pltpu
from jax.sharding import PartitionSpec as P

KMAX = 73
BLOCK = 128
LANES = 128
BOX = 160
SLOTS = 256
kinetic_unit = 0.5 * (2.0 * math.pi / 58.6) ** 2
f32, bf16, i32 = jnp.float32, jnp.bfloat16, jnp.int32


def dft_table(length, sign):
    steps = np.arange(length, dtype=np.int32)
    product = steps[:, None] * steps[None, :] % length
    angles = product.astype(np.float32) * np.float32(2.0 * math.pi / length)
    root = np.float32(math.sqrt(length))
    cosines = np.cos(angles) / root
    sines = np.float32(sign) * np.sin(angles) / root
    return np.stack([np.stack([cosines, sines], 1), np.stack([-sines, cosines], 1)], 0).astype(np.float32)


def box_half(grid_x, grid_y, ncolumns):
    freq_x = np.arange(grid_x) - grid_x * (np.arange(grid_x) >= grid_x // 2)
    freq_y = np.arange(grid_y) - grid_y * (np.arange(grid_y) >= grid_y // 2)
    radius_sq = np.sort((freq_x[:, None] ** 2 + freq_y[None, :] ** 2).ravel())
    return int(math.isqrt(int(radius_sq[ncolumns - 1])))


def make_tables(grid_z, grid_x, grid_y, z_local, half):
    count = grid_z // z_local
    width = 2 * half + 1
    fwd_z, back_z = dft_table(grid_z, 1.0), dft_table(grid_z, -1.0)
    fwd_x, back_x = dft_table(grid_x, 1.0), dft_table(grid_x, -1.0)
    fwd_y, back_y = dft_table(grid_y, 1.0), dft_table(grid_y, -1.0)
    box_x = (np.arange(width) - half) % grid_x
    box_y = (np.arange(width) - half) % grid_y
    zf = np.zeros((count, 8, 2 * grid_z), np.float32)
    zb = np.zeros((2 * grid_z, count, 8), np.float32)
    for d in range(2):
        for plane in range(z_local):
            w = np.arange(count) * z_local + plane
            zf[:, d * z_local + plane, :] = fwd_z[:, :, d, w].reshape(2 * grid_z, count).T
            zb[:, :, d * z_local + plane] = back_z[d, w].reshape(count, 2 * grid_z).T
    yf = np.zeros((2, BOX, 2, 256), np.float32)
    yf[:, :width, :, :grid_y] = fwd_y[:, box_y]
    xf = np.zeros((2, 2 * grid_x, BOX), np.float32)
    order = np.concatenate([np.arange(0, grid_x, 2), np.arange(1, grid_x, 2)])
    for c in range(2):
        xf[c, :, :width] = fwd_x[c, box_x][:, :, order].reshape(width, 2 * grid_x).T
    xb = np.zeros((2, BOX, 2, grid_x), np.float32)
    for c in range(2):
        for d in range(2):
            xb[d, :width, c] = back_x[c, order][:, d, box_x].T
    yb = np.zeros((2, 256, 2, BOX), np.float32)
    yb[:, :grid_y, :, :width] = back_y[:, :, :, box_y]
    arrays = (
        zf.reshape(count * 8, -1), zb.reshape(2 * grid_z, -1), yf.reshape(2, BOX, 512), xf,
        xb.reshape(2 * BOX, 2 * grid_x), yb.transpose(2, 0, 1, 3),
    )
    return [jnp.asarray(a.astype(jnp.bfloat16)) for a in arrays]


def dot(a, b, dims=((1,), (0,))):
    return lax.dot_general(a, b, (dims, ((), ())), preferred_element_type=f32)


def split3(x):
    hi = x.astype(bf16)
    rest = x - hi.astype(f32)
    mid = rest.astype(bf16)
    low = (rest - mid.astype(f32)).astype(bf16)
    return hi, mid, low


def iota(shape, axis):
    return lax.broadcasted_iota(i32, shape, axis)


def ones_where(mask):
    return jnp.where(mask, 1.0, 0.0).astype(bf16)


def quotient(values, divisor):
    return jnp.floor((values.astype(f32) + 0.5) * (1.0 / divisor)).astype(i32)


def frequencies(columns, grid_x, grid_y):
    x = quotient(columns, grid_y)
    y = columns - x * grid_y
    return jnp.where(x >= grid_x // 2, x - grid_x, x), jnp.where(y >= grid_y // 2, y - grid_y, y)


def radius_rows(p_ref, cm_ref, grid_x, grid_y, grid_z):
    own = cm_ref[pl.ds(2 * p_ref[0], 2), :]
    freq_x, freq_y = frequencies(own, grid_x, grid_y)
    flat = freq_x * freq_x + freq_y * freq_y
    row = iota((2 * grid_z, LANES), 0)
    z = jnp.where(row >= grid_z, row - grid_z, row)
    freq_z = jnp.where(z >= grid_z // 2, z - grid_z, z)
    sq = freq_z * freq_z
    return [sq + flat[h : h + 1, :] for h in range(2)]


def build(sizes):
    (grid_z, grid_x, grid_y, z_local, count, bands, natoms, nproj, entries, half) = sizes
    pairs = grid_x // 2
    blocks = z_local * grid_x * grid_y // BLOCK
    plane_blocks = blocks // z_local
    reach = natoms // count
    chunks = entries // LANES
    cj = 2 * nproj
    nch = 2 * z_local
    steps = 4

    def block_rows(values):
        plane = quotient(values, plane_blocks)
        rest = values - plane * plane_blocks
        k = quotient(rest, 3)
        return plane * plane_blocks + (rest - 3 * k) * pairs + k

    def slots_of(values, p):
        start = p * natoms // count - 2 * reach
        t = values - start
        t = jnp.where(t < 0, t + natoms, t)
        return jnp.where(t >= natoms, t - natoms, t)

    def columns_of(rows):
        padded = jnp.concatenate([rows.astype(f32), jnp.zeros((8 - chunks, LANES), f32)], 0)
        return padded.T.astype(i32)

    def slot_onehot(at_ref, p):
        cols = columns_of(slots_of(at_ref[...], p))
        lane = iota((LANES, SLOTS), 1)
        return jnp.concatenate([ones_where(lane == cols[:, i : i + 1]) for i in range(chunks)], 0)

    def spread_projectors(proj_ref, pf_ref):
        pf_ref[...] = proj_ref[...].astype(f32).reshape(entries * nproj, BLOCK)

    def box_indices(cm_ref, xi_ref, yi_ref):
        freq_x, freq_y = frequencies(cm_ref[...], grid_x, grid_y)
        xi_ref[...] = freq_x + half
        yi_ref[...] = freq_y + half

    def to_columns(p_ref, cm_ref, orb_ref, tab_ref, out_ref):
        radius = radius_rows(p_ref, cm_ref, grid_x, grid_y, grid_z)
        parts = []
        for h in range(2):
            values = orb_ref[:, h * LANES : (h + 1) * LANES].astype(f32)
            parts.append(jnp.where(radius[h] <= KMAX * KMAX, values, 0.0).astype(bf16))
        z = dot(tab_ref[...], jnp.concatenate(parts, 1))
        out = [z[:, h * LANES : (h + 1) * LANES].reshape(count, 8, LANES) for h in range(2)]
        out_ref[...] = jnp.concatenate(out, 1).astype(bf16)

    def forward(p_ref, cm_ref, zr_ref, yf_ref, xf_ref, bi_ref, at_ref, proj_ref,
                rs_ref, win_ref, send_ref, xi_ref, yi_ref, acc_ref, pf_ref):
        p = p_ref[0]
        box_indices(cm_ref, xi_ref, yi_ref)
        acc_ref[...] = jnp.zeros_like(acc_ref)
        box_row = iota((BOX, LANES), 0)

        def add_columns(step, carry):
            xrows = xi_ref[pl.ds(pl.multiple_of(step * 2 * steps, 8), 2 * steps), :]
            yrows = yi_ref[pl.ds(pl.multiple_of(step * 2 * steps, 8), 2 * steps), :]
            left, right = [], []
            for s in range(steps):
                v = zr_ref[step * steps + s].astype(f32)
                for h in range(2):
                    r = 2 * s + h
                    hot = ones_where(box_row == xrows[r : r + 1, :]).reshape(BOX // 16, 16, LANES)
                    right.append(ones_where(box_row == yrows[r : r + 1, :]))
                    rows = []
                    for ch in range(nch):
                        one = v[h * 8 + ch : h * 8 + ch + 1, :]
                        wide = jnp.broadcast_to(one, (16, LANES)).astype(bf16)
                        rows.append((hot * wide[None]).reshape(BOX, LANES))
                    left.append(jnp.concatenate(rows, 0))
            acc_ref[...] += dot(jnp.concatenate(left, 1), jnp.concatenate(right, 1), ((1,), (1,)))
            return carry

        lax.fori_loop(0, count // steps, add_columns, 0)
        rows = z_local * BOX
        ydone = dot(acc_ref[0:rows, :].astype(bf16), yf_ref[0]) + dot(
            acc_ref[rows : 2 * rows, :].astype(bf16), yf_ref[1]
        )
        ydone = ydone.astype(bf16)
        lane = iota((pairs, LANES), 1)
        for plane in range(z_local):
            mine = ydone[plane * BOX : (plane + 1) * BOX]
            real = dot(xf_ref[0], mine[:, 0:256]) + dot(xf_ref[1], mine[:, 256:512])
            for d in range(2):
                even = real[d * grid_x : d * grid_x + pairs]
                odd = real[d * grid_x + pairs : (d + 1) * grid_x]
                turned = pltpu.roll(odd[:, 0:128], 64, 1)
                middle = jnp.where(lane < 64, even[:, 128:256], turned)
                last = jnp.where(lane < 64, turned, pltpu.roll(odd[:, 128:256], 64, 1))
                for t, piece in enumerate((even[:, 0:128], middle, last)):
                    at = plane * plane_blocks + t * pairs
                    rs_ref[at : at + pairs, d * BLOCK : (d + 1) * BLOCK] = piece.astype(bf16)
        spread_projectors(proj_ref, pf_ref)
        cols = columns_of(block_rows(bi_ref[...]))
        block_lane = iota((LANES, blocks), 1)
        hot = jnp.concatenate(
            [ones_where(block_lane == cols[:, i : i + 1]) for i in range(chunks)], 0
        )
        picked = dot(hot, rs_ref[...])
        select_row = iota((2 * BLOCK, LANES), 0)
        select_lane = iota((2 * BLOCK, LANES), 1)
        corr = jnp.zeros((entries, LANES), f32)
        for j in range(nproj):
            values = pf_ref[pl.ds(j, entries, stride=nproj), :]
            product = jnp.concatenate([values, values], 1) * picked
            hi = product.astype(bf16)
            low = (product - hi.astype(f32)).astype(bf16)
            target = jnp.where(select_row >= BLOCK, nproj + j, j)
            ones = ones_where(select_lane == target)
            corr = corr + (dot(hi, ones) + dot(low, ones))
        pieces = jnp.concatenate(split3(corr), 1)
        window = dot(pieces, slot_onehot(at_ref, p), ((0,), (0,)))
        window = window[0:cj] + window[LANES : LANES + cj] + window[2 * LANES : 2 * LANES + cj]
        win_ref[...] = window
        send_ref[...] = jnp.zeros_like(send_ref)
        home = p * natoms // count
        for s in range(1, 5):
            up = lax.rem(p + s, count)
            ahead = up * natoms // count - home
            ahead = jnp.where(ahead < 0, ahead + natoms, ahead)
            send_ref[up] = pltpu.roll(window, SLOTS - ahead, 1)[:, 0:LANES]
            down = lax.rem(p - s + count, count)
            send_ref[down] = window[:, 0:LANES]

    def backward(p_ref, cm_ref, xr_ref, win_ref, rs_ref, pot_ref, coup_ref, bi_ref, at_ref, proj_ref,
                 xb_ref, yb_ref, zall_ref, oall_ref, out_ref,
                 xi_ref, yi_ref, pf_ref, grid_ref, ret_ref, pot_first, pot_rest):
        p = p_ref[0]
        pot_first[...] = pot_ref[:, :, 0:LANES].reshape(z_local * grid_x, LANES)
        pot_rest[:, 0 : grid_y - LANES] = pot_ref[:, :, LANES:grid_y].reshape(
            z_local * grid_x, grid_y - LANES
        )
        home = p * natoms // count
        spread_projectors(proj_ref, pf_ref)
        total = win_ref[...]
        nothing = jnp.zeros((cj, LANES), f32)
        for s in range(1, 5):
            down = lax.rem(p - s + count, count)
            total = total + jnp.concatenate([xr_ref[down], nothing], 1)
            up = lax.rem(p + s, count)
            ahead = up * natoms // count - home
            ahead = jnp.where(ahead < 0, ahead + natoms, ahead)
            total = total + pltpu.roll(jnp.concatenate([xr_ref[up], nothing], 1), ahead, 1)
        start = home - 2 * reach
        atom = start + iota((natoms, SLOTS), 1)
        atom = jnp.where(atom < 0, atom + natoms, atom)
        atom = jnp.where(atom >= natoms, atom - natoms, atom)
        select = ones_where(atom == iota((natoms, SLOTS), 0))
        near = dot(jnp.concatenate(split3(coup_ref[...]), 0), select)
        square = nproj * nproj
        near = near[0:square] + near[square : 2 * square] + near[2 * square : 3 * square]
        near = near.reshape(nproj, nproj, SLOTS)
        weight = jnp.concatenate(
            [jnp.sum(near * total[c * nproj : (c + 1) * nproj][None], 1) for c in range(2)], 0
        ).astype(bf16)
        ent_weight = dot(slot_onehot(at_ref, p), weight, ((1,), (1,)))
        terms = [jnp.zeros((entries, BLOCK), f32) for _ in range(2)]
        for j in range(nproj):
            values = pf_ref[pl.ds(j, entries, stride=nproj), :]
            for c in range(2):
                terms[c] = terms[c] + ent_weight[:, c * nproj + j : c * nproj + j + 1] * values
        pieces = jnp.concatenate(split3(jnp.concatenate(terms, 1)), 1)
        rows = block_rows(bi_ref[...])
        block_row = iota((blocks, LANES), 0)
        hot = jnp.concatenate(
            [ones_where(block_row == rows[i : i + 1, :]) for i in range(chunks)], 1
        )
        nonlocal_part = dot(hot, pieces)
        nonlocal_part = (
            nonlocal_part[:, 0:256] + nonlocal_part[:, 256:512] + nonlocal_part[:, 512:768]
        )
        lane = iota((pairs, LANES), 1)
        backs = [[], []]
        for plane in range(z_local):
            at = plane * plane_blocks
            even, odd = (
                [
                    part[pl.ds(plane * grid_x + parity, pairs, stride=2), :]
                    for part in (pot_first, pot_rest)
                ]
                for parity in range(2)
            )
            turned = pltpu.roll(odd[0], 64, 1)
            pot = (
                even[0],
                jnp.where(lane < 64, even[1], turned),
                jnp.where(lane < 64, turned, pltpu.roll(odd[1], 64, 1)),
            )
            stacked = []
            for c in range(2):
                h = []
                for t in range(3):
                    own = slice(at + t * pairs, at + (t + 1) * pairs)
                    lanes = slice(c * BLOCK, (c + 1) * BLOCK)
                    h.append(pot[t] * rs_ref[own, lanes].astype(f32) + nonlocal_part[own, lanes])
                swung = pltpu.roll(h[2], 64, 1)
                stacked.append(jnp.concatenate([h[0], jnp.where(lane < 64, h[1], 0.0)], 1))
                stacked.append(
                    jnp.concatenate(
                        [
                            jnp.where(lane < 64, pltpu.roll(h[1], 64, 1), swung),
                            jnp.where(lane < 64, swung, 0.0),
                        ],
                        1,
                    )
                )
            x_back = dot(xb_ref[...], jnp.concatenate(stacked, 0).astype(bf16)).astype(bf16)
            for c in range(2):
                backs[c].append(x_back[c * BOX : (c + 1) * BOX])
        backs = [jnp.concatenate(b, 0) for b in backs]
        rows_d = z_local * BOX
        for d in range(2):
            y_back = dot(backs[0], yb_ref[d, 0]) + dot(backs[1], yb_ref[d, 1])
            grid_ref[d * rows_d : (d + 1) * rows_d, :] = y_back.astype(bf16)
        box_indices(cm_ref, xi_ref, yi_ref)
        box_row = iota((BOX, LANES), 0)
        blank = jnp.zeros((8 - nch, LANES), f32)

        def take_columns(step, carry):
            base = pl.multiple_of(step * 8, 8)
            xrows = xi_ref[pl.ds(base, 8), :]
            yrows = yi_ref[pl.ds(base, 8), :]
            sums = list(carry)
            for s in range(4):
                hot_y = jnp.concatenate(
                    [ones_where(box_row == yrows[2 * s + h : 2 * s + h + 1, :]) for h in range(2)], 1
                )
                taken = dot(grid_ref[...], hot_y)
                halves, swapped = [], []
                for h in range(2):
                    mask = box_row == xrows[2 * s + h : 2 * s + h + 1, :]
                    rows = []
                    for ch in range(nch):
                        part = taken[ch * BOX : (ch + 1) * BOX, h * LANES : (h + 1) * LANES]
                        row = jnp.sum(jnp.where(mask, part, 0.0), 0, keepdims=True)
                        rows.append(row)
                    halves.append(jnp.concatenate(rows + [blank], 0))
                    other = rows[z_local:] + [-r for r in rows[:z_local]]
                    swapped.append(jnp.concatenate(other + [blank], 0))
                ret = jnp.concatenate(halves, 0)
                cross = jnp.concatenate(swapped, 0)
                ret_ref[step * 4 + s] = ret
                for m in range(bands):
                    other = zall_ref[m, step * 4 + s].astype(f32)
                    sums[m] = sums[m] + other * ret
                    sums[bands + m] = sums[bands + m] + other * cross
            return tuple(sums)

        zero = jnp.zeros((16, LANES), f32)
        sums = lax.fori_loop(0, count // 4, take_columns, (zero,) * (2 * bands))
        radius = radius_rows(p_ref, cm_ref, grid_x, grid_y, grid_z)
        band = p_ref[1]
        kin = [jnp.zeros((1, LANES), f32) for _ in range(2 * bands)]
        for h in range(2):
            lanes = slice(h * LANES, (h + 1) * LANES)
            own = oall_ref[band, :, lanes].astype(f32)
            kinetic = jnp.where(radius[h] <= KMAX * KMAX, kinetic_unit * radius[h].astype(f32), 0.0)
            own = kinetic * own
            for m in range(bands):
                other = oall_ref[m, :, lanes].astype(f32)
                kin[m] = kin[m] + jnp.sum(other * own, 0, keepdims=True)
                kin[bands + m] = kin[bands + m] + jnp.sum(
                    other[:grid_z] * own[grid_z:] - other[grid_z:] * own[:grid_z], 0, keepdims=True
                )
        lane = iota((1, LANES), 1)
        row = jnp.zeros((1, LANES), f32)
        for n in range(2 * bands):
            value = jnp.sum(sums[n], 0, keepdims=True) + kin[n]
            value = jnp.sum(value, 1, keepdims=True)
            for k, piece in enumerate(split3(value)):
                row = jnp.where(lane == 2 * bands * k + n, piece.astype(f32), row)
        sub = iota((16, LANES), 0)
        carried = jnp.where(sub == nch, jnp.broadcast_to(row, (16, LANES)), 0.0)
        out_ref[...] = (ret_ref[...] + carried[None]).astype(bf16)

    def finish(p_ref, cm_ref, orb_ref, rr_ref, tab_ref, applied_ref, sub_ref):
        radius = radius_rows(p_ref, cm_ref, grid_x, grid_y, grid_z)
        got = rr_ref[...].astype(f32)
        right = jnp.concatenate(
            [got[:, h * 8 : (h + 1) * 8].reshape(count * 8, LANES) for h in range(2)], 1
        ).astype(bf16)
        z_back = dot(tab_ref[...], right)
        for h in range(2):
            lanes = slice(h * LANES, (h + 1) * LANES)
            values = orb_ref[:, lanes].astype(f32)
            result = kinetic_unit * radius[h].astype(f32) * values + z_back[:, lanes]
            applied_ref[:, lanes] = jnp.where(radius[h] <= KMAX * KMAX, result, 0.0)
        summed = jnp.sum(got[:, 0:8], 0)
        summed = summed + (
            pltpu.roll(summed, LANES - 2 * bands, 1) + pltpu.roll(summed, LANES - 4 * bands, 1)
        )
        sub_ref[...] = summed * (1.0 / (grid_z * count * 2 * LANES))

    return to_columns, forward, backward, finish


def call(kernel, out_shape, n_scalar, n_in, scratch=()):
    smem = pl.BlockSpec(memory_space=pltpu.SMEM)
    vmem = pl.BlockSpec(memory_space=pltpu.VMEM)
    multiple = isinstance(out_shape, (list, tuple))
    return pl.pallas_call(
        kernel,
        out_shape=out_shape,
        in_specs=[smem] * n_scalar + [vmem] * n_in,
        out_specs=[vmem] * len(out_shape) if multiple else vmem,
        scratch_shapes=list(scratch),
        compiler_params=pltpu.CompilerParams(vmem_limit_bytes=56 * 1024 * 1024),
    )


def per_device(orbitals, column_map, potential, projectors, block_index, block_atom, coupling):
    _, _, grid_z, col_local = orbitals.shape
    z_local, grid_x, grid_y = potential.shape
    natoms, nproj = coupling.shape[0], coupling.shape[1]
    entries = block_index.shape[0]
    count, bands = lax.axis_size("pw"), lax.axis_size("band")
    ncolumns = column_map.shape[0]
    half = box_half(grid_x, grid_y, ncolumns)
    zf, zb, yf, xf, xb, yb = make_tables(grid_z, grid_x, grid_y, z_local, half)
    sizes = (grid_z, grid_x, grid_y, z_local, count, bands, natoms, nproj, entries, half)
    to_columns, forward, backward, finish = build(sizes)
    shape = jax.ShapeDtypeStruct
    blocks = z_local * grid_x * grid_y // BLOCK
    cj = 2 * nproj

    place = jnp.stack([lax.axis_index("pw"), lax.axis_index("band")]).astype(i32)
    cm = column_map.reshape(ncolumns // LANES, LANES)
    orb = orbitals.reshape(2 * grid_z, col_local)
    bi = block_index.reshape(entries // LANES, LANES)
    at = block_atom.reshape(entries // LANES, LANES)
    coup = coupling.reshape(natoms, nproj * nproj).T
    packet = (count, 16, LANES)

    sent = call(to_columns, shape(packet, bf16), 1, 3)(place, cm, orb, zf)
    planes = lax.all_to_all(sent, "pw", split_axis=0, concat_axis=0, tiled=True)
    index_scratch = [pltpu.VMEM(cm.shape, i32), pltpu.VMEM(cm.shape, i32)]
    pf_scratch = pltpu.VMEM((entries * nproj, BLOCK), f32)
    real_space, window, to_send = call(
        forward,
        (shape((blocks, 2 * BLOCK), bf16), shape((cj, SLOTS), f32), shape((count, cj, LANES), f32)),
        1, 7,
        index_scratch + [pltpu.VMEM((2 * z_local * BOX, BOX), f32), pf_scratch],
    )(place, cm, planes, yf, xf, bi, at, projectors)
    other = lax.all_to_all(to_send, "pw", split_axis=0, concat_axis=0, tiled=True)
    all_planes = lax.all_gather(planes, "band", axis=0, tiled=False)
    all_orb = lax.all_gather(orb, "band", axis=0, tiled=False)
    back = call(
        backward, shape(packet, bf16), 1, 13,
        index_scratch
        + [pf_scratch, pltpu.VMEM((2 * z_local * BOX, BOX), bf16), pltpu.VMEM(packet, f32)]
        + [pltpu.VMEM((z_local * grid_x, LANES), f32)] * 2,
    )(place, cm, other, window, real_space, potential, coup, bi, at, projectors, xb, yb, all_planes, all_orb)
    returned = lax.all_to_all(back, "pw", split_axis=0, concat_axis=0, tiled=True)
    applied, sums = call(
        finish, (shape((2 * grid_z, col_local), f32), shape((8, LANES), f32)), 1, 4
    )(place, cm, orb, returned, zb)
    applied = applied.reshape(1, 2, grid_z, col_local)
    subspace = sums[2 * z_local, : 2 * bands].reshape(2, bands, 1)
    return applied, subspace


def solution(mesh):
    in_specs = (
        P("band", None, None, "pw"),
        P(),
        P("pw", None, None),
        P("pw", None, None),
        P("pw"),
        P("pw"),
        P(),
    )
    out_specs = (P("band", None, None, "pw"), P(None, None, "band"))
    return jax.shard_map(
        per_device, mesh=mesh, in_specs=in_specs, out_specs=out_specs, check_vma=False
    )
```

profile of v0, /device:TPU:6, one launch (start us, length us, event | category | flops | bytes accessed | tf_op | source)
XLA Modules:
  0.0 133.7 jit_solution(8859322369338759409)
XLA Ops:
  7.2 0.0 all-gather.3.cloned.1.call-start
  7.2 0.6 pad_add_fusion.p_ref
  7.8 2.2 %shard_map.140 = bf16[64,16,128]{2,1,0:T(8,128)(2,1)} custom-call(s32[2]{0:T(128)} %pad_add_fusion.p_ref, s32[128,128]{1,0:T(8,128)} %bitcast.16, bf16[384,256]{1,0:T(8,128)(2,1)} %bitcast.13, bf16[512,384]{1,0:T(8,128)(2,1)} %constant.21.clone.tab_ref), custom_call_target="tpu_custom_call" | custom-call | tf_op jit(solution)/shard_map/pallas_call | solution.py:448
  10.0 28.4 %all_to_all.15.zr_ref = bf16[64,16,128]{2,1,0:T(8,128)(2,1)} all-to-all(bf16[64,16,128]{2,1,0:T(8,128)(2,1)} %shard_map.140), channel_id=1, replica_groups=mesh['band'=4,'pw'=64] {'pw'}, dimensions={0} | all-to-all | bytes 524288 | tf_op jit(solution)/shard_map/all_to_all | solution.py:449
  38.4 0.0 all-gather.3.cloned.1.call-update
  38.4 17.1 %shard_map.141 = (bf16[864,256]{1,0:T(8,128)(2,1)}, f32[16,256]{1,0:T(8,128)}, f32[64,16,128]{2,1,0:T(8,128)}) custom-call(s32[2]{0:T(128)} %pad_add_fusion.p_ref, s32[128,128]{1,0:T(8,128)} %bitcast.17, bf16[64,16,128]{2,1,0:T(8,128)(2,1)} %all_to_all.15.zr_ref, bf16[2,160,512]{2,1,0:T(8,128)(2,1)} %constant.23.clone.yf_ref, ...), custom_call_target="tpu_custom_call" | custom-call | tf_op jit(solution)/shard_map/pallas_call | solution.py:452
  55.5 0.0 copy-start.1
  55.5 5.9 %all-to-all-start.1 = ((f32[64,16,128]{2,1,0:T(8,128)}), f32[64,16,128]{2,1,0:T(8,128)S(1)}, u32[]{:S(2)}, u32[]{:S(2)}) async-start(f32[64,16,128]{2,1,0:T(8,128)} %get-tuple-element.7), calls=%async_computation.1 | async-start | bytes 1048576 | tf_op jit(solution)/shard_map/all_to_all | solution.py:458
  61.4 0.0 copy-done.1
  61.4 12.1 %all_gather.11.oall_ref = bf16[4,384,256]{2,1,0:T(8,128)(2,1)} all-gather(bf16[1,384,256]{2,1,0:T(8,128)(2,1)S(1)} %bitcast.15), channel_id=1, replica_groups=mesh['band'=4,'pw'=64] {'band'}, dimensions={0}, use_global_device_ids=true | all-gather | bytes 983040 | tf_op jit(solution)/shard_map/all_gather | solution.py:460
  73.4 6.0 %all-to-all-done.1.xr_ref = f32[64,16,128]{2,1,0:T(8,128)S(1)} async-done(((f32[64,16,128]{2,1,0:T(8,128)}), f32[64,16,128]{2,1,0:T(8,128)S(1)}, u32[]{:S(2)}, u32[]{:S(2)}) %all-to-all-start.1) | async-done | bytes 524320 | tf_op jit(solution)/shard_map/all_to_all | solution.py:458
  79.4 0.0 copy-start
  79.4 0.0 all-gather.3.cloned.1.call-done
  79.4 0.8 copy-done
  80.2 21.6 %shard_map.142 = bf16[64,16,128]{2,1,0:T(8,128)(2,1)} custom-call(s32[2]{0:T(128)} %pad_add_fusion.p_ref, s32[128,128]{1,0:T(8,128)} %bitcast.18, f32[64,16,128]{2,1,0:T(8,128)} %copy-done, f32[16,256]{1,0:T(8,128)} %get-tuple-element.8.win_ref, bf16[864,256]{1,0:T(8,128)(2,1)} %get-tuple-element.9.rs_ref, f32[3,192,192]{2,1,0:T(8,128)} %pot_ref.1, ...), custom_call_target="tpu_custom_call" | custom-call | tf_op jit(solution)/shard_map/pallas_call | solution.py:461
  101.9 21.4 %all_to_all.16.rr_ref = bf16[64,16,128]{2,1,0:T(8,128)(2,1)} all-to-all(bf16[64,16,128]{2,1,0:T(8,128)(2,1)} %shard_map.142), channel_id=1, replica_groups=mesh['band'=4,'pw'=64] {'pw'}, dimensions={0} | all-to-all | bytes 524288 | tf_op jit(solution)/shard_map/all_to_all | solution.py:467
  123.2 2.2 %shard_map.143 = (f32[384,256]{1,0:T(8,128)}, f32[8,128]{1,0:T(8,128)}) custom-call(s32[2]{0:T(128)} %pad_add_fusion.p_ref, s32[128,128]{1,0:T(8,128)} %bitcast.19, bf16[384,256]{1,0:T(8,128)(2,1)} %bitcast.14, bf16[64,16,128]{2,1,0:T(8,128)(2,1)} %all_to_all.16.rr_ref, bf16[384,512]{1,0:T(8,128)(2,1)} %constant.22.clone.tab_ref), custom_call_target="tpu_custom_call" | custom-call | tf_op jit(solution)/shard_map/pallas_call | solution.py:468
  125.5 0.7 slice_reduce_fusion
  126.2 0.6 reshape_squeeze.3
Async XLA Ops:
  7.2 72.3 %all-gather.3.cloned.1.call-start = ((), (), s32[]{:S(2)}) async-start(), calls=%async_computation.3 | async-start | bytes 1310720 | tf_op jit(solution)/shard_map/all_gather | solution.py:459
  55.5 5.9 %copy-start.1 = (bf16[1,2,192,256]{3,2,1,0:T(8,128)(2,1)S(1)}, bf16[1,2,192,256]{3,2,1,0:T(8,128)(2,1)}, u32[]{:S(2)}) copy-start(bf16[1,2,192,256]{3,2,1,0:T(8,128)(2,1)} %param.13) | copy-start | bytes 589828
  55.5 23.9 %all-to-all-start.1 = ((f32[64,16,128]{2,1,0:T(8,128)}), f32[64,16,128]{2,1,0:T(8,128)S(1)}, u32[]{:S(2)}, u32[]{:S(2)}) async-start(f32[64,16,128]{2,1,0:T(8,128)} %get-tuple-element.7), calls=%async_computation.1 | async-start | bytes 1048576 | tf_op jit(solution)/shard_map/all_to_all | solution.py:458
  79.4 0.8 copy-start
Sparse Core Ops, SparseCore 0:
  38.5 17.3 all-gather.2
where the time goes:
time: 134 us
  blocking collectives  61.8 us (46%)
  Pallas kernels  43.1 us (32%)
  between operations  14.1 us (11%)
  waiting for transfers between devices  6 us (4%)
  starting transfers between devices  5.9 us (4%)
  local copies, waits for them, and re-layouts  2.16 us (2%)
    all_to_all x1, blocking collectives, per_device(): planes = lax.all_to_all(sent, 'pw', split_axis=0, concat_axis=0, tiled=True)  28.4 us
    pallas_call x1, Pallas kernels, per_device(): call(backward, shape(packet, bf16), 1, 13, index_scratch + [pf_scratch, p...  21.6 us
    all_to_all x1, blocking collectives, per_device(): lax.all_to_all(back, 'pw', split_axis=0, concat_axis=0, tiled=True)  21.4 us
    pallas_call x1, Pallas kernels, per_device(): call(forward, (shape((blocks, 2 * BLOCK), bf16), shape((cj, SLOTS), f32),...  17.1 us
    all_gather x1, blocking collectives, per_device(): all_orb = lax.all_gather(orb, 'band', axis=0, tiled=False)  12.1 us
    all_to_all x1, waiting for transfers between devices, per_device(): lax.all_to_all(to_send, 'pw', split_axis=0, concat_axis=0, tiled=True)  5.98 us
    all_to_all x1, starting transfers between devices, per_device(): lax.all_to_all(to_send, 'pw', split_axis=0, concat_axis=0, tiled=True)  5.86 us
  transfers between devices with their start and end apart: 2, of which 1 were waited for; matrix products, arithmetic and copies ran while one was open for 0% of the time, Pallas kernels for 13%

commit v1 on v0

--- a/solution.py
+++ b/solution.py
@@ -11,7 +11,9 @@
 KMAX = 73
 BLOCK = 128
 LANES = 128
-BOX = 160
+VMEM_MIB, ALL_MIB = 52, 58
+MAIN, TAIL = 80, 16
+PACK = MAIN + TAIL
 SLOTS = 256
 kinetic_unit = 0.5 * (2.0 * math.pi / 58.6) ** 2
 f32, bf16, i32 = jnp.float32, jnp.bfloat16, jnp.int32
@@ -49,22 +51,34 @@
             w = np.arange(count) * z_local + plane
             zf[:, d * z_local + plane, :] = fwd_z[:, :, d, w].reshape(2 * grid_z, count).T
             zb[:, :, d * z_local + plane] = back_z[d, w].reshape(count, 2 * grid_z).T
-    yf = np.zeros((2, BOX, 2, 256), np.float32)
-    yf[:, :width, :, :grid_y] = fwd_y[:, box_y]
-    xf = np.zeros((2, 2 * grid_x, BOX), np.float32)
+    split = LANES
+    more = width - split
+    pair = [np.arange(par, width, 2) for par in range(2)]
+    beyond = [np.arange(split + par, width, 2) for par in range(2)]
+    yf = np.zeros((2, split, 2, 256), np.float32)
+    yf[:, :, :, :grid_y] = fwd_y[:, box_y[:split]]
+    yft = np.zeros((2, 2, TAIL, 2, 256), np.float32)
+    xf = np.zeros((2 * grid_x, 2, 2, MAIN), np.float32)
+    xb = np.zeros((2, 2, MAIN, 2, grid_x), np.float32)
     order = np.concatenate([np.arange(0, grid_x, 2), np.arange(1, grid_x, 2)])
-    for c in range(2):
-        xf[c, :, :width] = fwd_x[c, box_x][:, :, order].reshape(width, 2 * grid_x).T
-    xb = np.zeros((2, BOX, 2, grid_x), np.float32)
-    for c in range(2):
-        for d in range(2):
-            xb[d, :width, c] = back_x[c, order][:, d, box_x].T
-    yb = np.zeros((2, 256, 2, BOX), np.float32)
-    yb[:, :grid_y, :, :width] = back_y[:, :, :, box_y]
+    yb = np.zeros((2, 256, 2, split), np.float32)
+    yb[:, :grid_y] = back_y[:, :, :, box_y[:split]]
+    ybt = np.zeros((2, 2, 2, TAIL, 256), np.float32)
+    for par in range(2):
+        xs, ys = box_x[pair[par]], box_y[beyond[par]]
+        yft[:, par, : len(ys), :, :grid_y] = fwd_y[:, ys]
+        for c in range(2):
+            xf[:, c, par, : len(xs)] = fwd_x[c, xs][:, :, order].reshape(len(xs), 2 * grid_x).T
+            for d in range(2):
+                xb[d, par, : len(xs), c] = back_x[c, order][:, d, xs].T
+                ybt[c, d, par, : len(ys), :grid_y] = back_y[c, :, d, ys]
     arrays = (
-        zf.reshape(count * 8, -1), zb.reshape(2 * grid_z, -1), yf.reshape(2, BOX, 512), xf,
-        xb.reshape(2 * BOX, 2 * grid_x), yb.transpose(2, 0, 1, 3),
+        zf.reshape(count * 8, -1), zb.reshape(2 * grid_z, -1), yf.reshape(2 * split, 512),
+        yft.reshape(4 * TAIL, 512), xf.reshape(2 * grid_x, 4 * MAIN), xb.reshape(4 * MAIN, 2 * grid_x),
+        yb.reshape(2, 256, 2 * split), ybt.reshape(2, 4 * TAIL, 256),
     )
+    reach_x = math.isqrt((half + 1) ** 2 - 1 - (split - half) ** 2)
+    assert (half + reach_x) // 2 < 64 and (more + 1) // 2 <= TAIL and half + 1 <= MAIN
     return [jnp.asarray(a.astype(jnp.bfloat16)) for a in arrays]
 
 
@@ -98,8 +112,8 @@
     return jnp.where(x >= grid_x // 2, x - grid_x, x), jnp.where(y >= grid_y // 2, y - grid_y, y)
 
 
-def radius_rows(p_ref, cm_ref, grid_x, grid_y, grid_z):
-    own = cm_ref[pl.ds(2 * p_ref[0], 2), :]
+def radius_rows(p, cm_ref, grid_x, grid_y, grid_z):
+    own = cm_ref[pl.ds(2 * p, 2), :]
     freq_x, freq_y = frequencies(own, grid_x, grid_y)
     flat = freq_x * freq_x + freq_y * freq_y
     row = iota((2 * grid_z, LANES), 0)
@@ -118,7 +132,9 @@
     chunks = entries // LANES
     cj = 2 * nproj
     nch = 2 * z_local
-    steps = 4
+    steps = 16
+    gsteps = 8
+    rows_c = z_local * PACK
 
     def block_rows(values):
         plane = quotient(values, plane_blocks)
@@ -141,30 +157,44 @@
         lane = iota((LANES, SLOTS), 1)
         return jnp.concatenate([ones_where(lane == cols[:, i : i + 1]) for i in range(chunks)], 0)
 
-    def spread_projectors(proj_ref, pf_ref):
-        pf_ref[...] = proj_ref[...].astype(f32).reshape(entries * nproj, BLOCK)
-
-    def box_indices(cm_ref, xi_ref, yi_ref):
+    def box_indices(cm_ref, row_ref, lane_ref):
         freq_x, freq_y = frequencies(cm_ref[...], grid_x, grid_y)
-        xi_ref[...] = freq_x + half
-        yi_ref[...] = freq_y + half
-
-    def to_columns(p_ref, cm_ref, orb_ref, tab_ref, out_ref):
-        radius = radius_rows(p_ref, cm_ref, grid_x, grid_y, grid_z)
+        x, y = freq_x + half, freq_y + half
+        pair, parity, more = x >> 1, x & 1, y - LANES
+        row_ref[...] = jnp.where(more >= 0, MAIN + (more >> 1), pair)
+        lane_ref[...] = jnp.where(
+            more >= 0, (more & 1) * LANES + parity * 64 + pair, parity * LANES + y
+        )
+
+    def near_coupling(p, coup):
+        start = p * natoms // count - 2 * reach
+        atom = start + iota((natoms, SLOTS), 1)
+        atom = jnp.where(atom < 0, atom + natoms, atom)
+        atom = jnp.where(atom >= natoms, atom - natoms, atom)
+        select = ones_where(atom == iota((natoms, SLOTS), 0))
+        near = dot(jnp.concatenate(split3(coup()[...]), 0), select)
+        square = nproj * nproj
+        return near[0:square] + near[square : 2 * square] + near[2 * square : 3 * square]
+
+    def to_columns(cm, orb, table, out_ref):
+        p = lax.axis_index("pw")
+        radius = radius_rows(p, cm(), grid_x, grid_y, grid_z)
+        orb_ref = orb()
         parts = []
         for h in range(2):
             values = orb_ref[:, h * LANES : (h + 1) * LANES].astype(f32)
             parts.append(jnp.where(radius[h] <= KMAX * KMAX, values, 0.0).astype(bf16))
-        z = dot(tab_ref[...], jnp.concatenate(parts, 1))
+        z = dot(table()[...], jnp.concatenate(parts, 1))
         out = [z[:, h * LANES : (h + 1) * LANES].reshape(count, 8, LANES) for h in range(2)]
         out_ref[...] = jnp.concatenate(out, 1).astype(bf16)
 
-    def forward(p_ref, cm_ref, zr_ref, yf_ref, xf_ref, bi_ref, at_ref, proj_ref,
-                rs_ref, win_ref, send_ref, xi_ref, yi_ref, acc_ref, pf_ref):
-        p = p_ref[0]
-        box_indices(cm_ref, xi_ref, yi_ref)
+    def forward(cm, zr_ref, yf, yft, xf, bi, at, proj, coup,
+                rs_ref, win_ref, send_ref, near_ref, xi_ref, yi_ref, acc_ref, pf_ref):
+        p = lax.axis_index("pw")
+        box_indices(cm(), xi_ref, yi_ref)
         acc_ref[...] = jnp.zeros_like(acc_ref)
-        box_row = iota((BOX, LANES), 0)
+        pack_row = iota((PACK, LANES), 0)
+        pack_lane = iota((256, LANES), 0)
 
         def add_columns(step, carry):
             xrows = xi_ref[pl.ds(pl.multiple_of(step * 2 * steps, 8), 2 * steps), :]
@@ -174,27 +204,46 @@
                 v = zr_ref[step * steps + s].astype(f32)
                 for h in range(2):
                     r = 2 * s + h
-                    hot = ones_where(box_row == xrows[r : r + 1, :]).reshape(BOX // 16, 16, LANES)
-                    right.append(ones_where(box_row == yrows[r : r + 1, :]))
+                    hot = ones_where(pack_row == xrows[r : r + 1, :]).reshape(PACK // 16, 16, LANES)
+                    right.append(ones_where(pack_lane == yrows[r : r + 1, :]))
                     rows = []
                     for ch in range(nch):
                         one = v[h * 8 + ch : h * 8 + ch + 1, :]
                         wide = jnp.broadcast_to(one, (16, LANES)).astype(bf16)
-                        rows.append((hot * wide[None]).reshape(BOX, LANES))
+                        rows.append((hot * wide[None]).reshape(PACK, LANES))
                     left.append(jnp.concatenate(rows, 0))
             acc_ref[...] += dot(jnp.concatenate(left, 1), jnp.concatenate(right, 1), ((1,), (1,)))
             return carry
 
         lax.fori_loop(0, count // steps, add_columns, 0)
-        rows = z_local * BOX
-        ydone = dot(acc_ref[0:rows, :].astype(bf16), yf_ref[0]) + dot(
-            acc_ref[rows : 2 * rows, :].astype(bf16), yf_ref[1]
-        )
-        ydone = ydone.astype(bf16)
+        yf_ref, yft_ref, xf_ref = yf(), yft(), xf()
+        main, tails = [], []
+        for plane in range(z_local):
+            starts = [c * rows_c + plane * PACK for c in range(2)]
+            for par in range(2):
+                lanes = slice(par * LANES, (par + 1) * LANES)
+                main.append(jnp.concatenate([acc_ref[r : r + MAIN, lanes] for r in starts], 1))
+            tails.append(
+                jnp.concatenate(
+                    [
+                        acc_ref[r + MAIN : r + PACK, par * LANES : (par + 1) * LANES]
+                        for r in starts
+                        for par in range(2)
+                    ],
+                    0,
+                ).astype(bf16)
+            )
+        ydone = dot(jnp.concatenate(main, 0).astype(bf16), yf_ref[...])
         lane = iota((pairs, LANES), 1)
         for plane in range(z_local):
-            mine = ydone[plane * BOX : (plane + 1) * BOX]
-            real = dot(xf_ref[0], mine[:, 0:256]) + dot(xf_ref[1], mine[:, 256:512])
+            more = dot(tails[plane], yft_ref[...], ((0,), (0,)))
+            mine = []
+            for par in range(2):
+                r = (plane * 2 + par) * MAIN
+                mine.append(ydone[r : r + 64] + more[par * 64 : (par + 1) * 64])
+                mine.append(ydone[r + 64 : r + MAIN])
+            mine = jnp.concatenate(mine, 0).astype(bf16)
+            real = dot(xf_ref[...], jnp.concatenate([mine[:, 0:256], mine[:, 256:512]], 0))
             for d in range(2):
                 even = real[d * grid_x : d * grid_x + pairs]
                 odd = real[d * grid_x + pairs : (d + 1) * grid_x]
@@ -202,10 +251,11 @@
                 middle = jnp.where(lane < 64, even[:, 128:256], turned)
                 last = jnp.where(lane < 64, turned, pltpu.roll(odd[:, 128:256], 64, 1))
                 for t, piece in enumerate((even[:, 0:128], middle, last)):
-                    at = plane * plane_blocks + t * pairs
-                    rs_ref[at : at + pairs, d * BLOCK : (d + 1) * BLOCK] = piece.astype(bf16)
-        spread_projectors(proj_ref, pf_ref)
-        cols = columns_of(block_rows(bi_ref[...]))
+                    own = plane * plane_blocks + t * pairs
+                    rs_ref[own : own + pairs, d * BLOCK : (d + 1) * BLOCK] = piece.astype(bf16)
+        near_ref[...] = near_coupling(p, coup)
+        pf_ref[...] = proj()[...].astype(f32)
+        cols = columns_of(block_rows(bi()[...]))
         block_lane = iota((LANES, blocks), 1)
         hot = jnp.concatenate(
             [ones_where(block_lane == cols[:, i : i + 1]) for i in range(chunks)], 0
@@ -223,7 +273,7 @@
             ones = ones_where(select_lane == target)
             corr = corr + (dot(hi, ones) + dot(low, ones))
         pieces = jnp.concatenate(split3(corr), 1)
-        window = dot(pieces, slot_onehot(at_ref, p), ((0,), (0,)))
+        window = dot(pieces, slot_onehot(at(), p), ((0,), (0,)))
         window = window[0:cj] + window[LANES : LANES + cj] + window[2 * LANES : 2 * LANES + cj]
         win_ref[...] = window
         send_ref[...] = jnp.zeros_like(send_ref)
@@ -236,16 +286,11 @@
             down = lax.rem(p - s + count, count)
             send_ref[down] = window[:, 0:LANES]
 
-    def backward(p_ref, cm_ref, xr_ref, win_ref, rs_ref, pot_ref, coup_ref, bi_ref, at_ref, proj_ref,
-                 xb_ref, yb_ref, zall_ref, oall_ref, out_ref,
+    def backward(cm, xr_ref, win_ref, rs_ref, potential, near_ref, bi, at, proj,
+                 xb, yb, ybt, zall, oall, out_ref,
                  xi_ref, yi_ref, pf_ref, grid_ref, ret_ref, pot_first, pot_rest):
-        p = p_ref[0]
-        pot_first[...] = pot_ref[:, :, 0:LANES].reshape(z_local * grid_x, LANES)
-        pot_rest[:, 0 : grid_y - LANES] = pot_ref[:, :, LANES:grid_y].reshape(
-            z_local * grid_x, grid_y - LANES
-        )
+        p = lax.axis_index("pw")
         home = p * natoms // count
-        spread_projectors(proj_ref, pf_ref)
         total = win_ref[...]
         nothing = jnp.zeros((cj, LANES), f32)
         for s in range(1, 5):
@@ -255,26 +300,20 @@
             ahead = up * natoms // count - home
             ahead = jnp.where(ahead < 0, ahead + natoms, ahead)
             total = total + pltpu.roll(jnp.concatenate([xr_ref[up], nothing], 1), ahead, 1)
-        start = home - 2 * reach
-        atom = start + iota((natoms, SLOTS), 1)
-        atom = jnp.where(atom < 0, atom + natoms, atom)
-        atom = jnp.where(atom >= natoms, atom - natoms, atom)
-        select = ones_where(atom == iota((natoms, SLOTS), 0))
-        near = dot(jnp.concatenate(split3(coup_ref[...]), 0), select)
-        square = nproj * nproj
-        near = near[0:square] + near[square : 2 * square] + near[2 * square : 3 * square]
+        near = near_ref[...]
         near = near.reshape(nproj, nproj, SLOTS)
         weight = jnp.concatenate(
             [jnp.sum(near * total[c * nproj : (c + 1) * nproj][None], 1) for c in range(2)], 0
         ).astype(bf16)
-        ent_weight = dot(slot_onehot(at_ref, p), weight, ((1,), (1,)))
+        pf_ref[...] = proj()[...].astype(f32)
+        ent_weight = dot(slot_onehot(at(), p), weight, ((1,), (1,)))
         terms = [jnp.zeros((entries, BLOCK), f32) for _ in range(2)]
         for j in range(nproj):
             values = pf_ref[pl.ds(j, entries, stride=nproj), :]
             for c in range(2):
                 terms[c] = terms[c] + ent_weight[:, c * nproj + j : c * nproj + j + 1] * values
         pieces = jnp.concatenate(split3(jnp.concatenate(terms, 1)), 1)
-        rows = block_rows(bi_ref[...])
+        rows = block_rows(bi()[...])
         block_row = iota((blocks, LANES), 0)
         hot = jnp.concatenate(
             [ones_where(block_row == rows[i : i + 1, :]) for i in range(chunks)], 1
@@ -283,10 +322,16 @@
         nonlocal_part = (
             nonlocal_part[:, 0:256] + nonlocal_part[:, 256:512] + nonlocal_part[:, 512:768]
         )
+        pot_ref = potential()
+        pot_first[...] = pot_ref[:, :, 0:LANES].reshape(z_local * grid_x, LANES)
+        pot_rest[:, 0 : grid_y - LANES] = pot_ref[:, :, LANES:grid_y].reshape(
+            z_local * grid_x, grid_y - LANES
+        )
+        xb_ref, yb_ref, ybt_ref = xb(), yb(), ybt()
         lane = iota((pairs, LANES), 1)
         backs = [[], []]
         for plane in range(z_local):
-            at = plane * plane_blocks
+            first = plane * plane_blocks
             even, odd = (
                 [
                     part[pl.ds(plane * grid_x + parity, pairs, stride=2), :]
@@ -304,7 +349,7 @@
             for c in range(2):
                 h = []
                 for t in range(3):
-                    own = slice(at + t * pairs, at + (t + 1) * pairs)
+                    own = slice(first + t * pairs, first + (t + 1) * pairs)
                     lanes = slice(c * BLOCK, (c + 1) * BLOCK)
                     h.append(pot[t] * rs_ref[own, lanes].astype(f32) + nonlocal_part[own, lanes])
                 swung = pltpu.roll(h[2], 64, 1)
@@ -319,33 +364,52 @@
                     )
                 )
             x_back = dot(xb_ref[...], jnp.concatenate(stacked, 0).astype(bf16)).astype(bf16)
+            tail = jnp.zeros((4 * TAIL, LANES), f32)
             for c in range(2):
-                backs[c].append(x_back[c * BOX : (c + 1) * BOX])
-        backs = [jnp.concatenate(b, 0) for b in backs]
-        rows_d = z_local * BOX
-        for d in range(2):
-            y_back = dot(backs[0], yb_ref[d, 0]) + dot(backs[1], yb_ref[d, 1])
-            grid_ref[d * rows_d : (d + 1) * rows_d, :] = y_back.astype(bf16)
+                mine = x_back[c * 2 * MAIN : (c + 1) * 2 * MAIN]
+                backs[c].append(mine)
+                near_rows = jnp.concatenate([mine[0:64], mine[MAIN : MAIN + 64]], 0)
+                tail = tail + dot(ybt_ref[c], near_rows, ((1,), (1,)))
+            for d in range(2):
+                for par in range(2):
+                    r = d * rows_c + plane * PACK + MAIN
+                    own = (2 * d + par) * TAIL
+                    grid_ref[r : r + TAIL, par * LANES : (par + 1) * LANES] = tail[
+                        own : own + TAIL
+                    ].astype(bf16)
+        y_back = dot(jnp.concatenate(backs[0], 0), yb_ref[0]) + dot(
+            jnp.concatenate(backs[1], 0), yb_ref[1]
+        )
+        for plane in range(z_local):
+            for par in range(2):
+                own = (plane * 2 + par) * MAIN
+                for d in range(2):
+                    r = d * rows_c + plane * PACK
+                    grid_ref[r : r + MAIN, par * LANES : (par + 1) * LANES] = y_back[
+                        own : own + MAIN, d * LANES : (d + 1) * LANES
+                    ].astype(bf16)
+        cm_ref, zall_ref = cm(), zall()
         box_indices(cm_ref, xi_ref, yi_ref)
-        box_row = iota((BOX, LANES), 0)
+        pack_row = iota((PACK, LANES), 0)
+        pack_lane = iota((256, LANES), 0)
         blank = jnp.zeros((8 - nch, LANES), f32)
 
         def take_columns(step, carry):
-            base = pl.multiple_of(step * 8, 8)
-            xrows = xi_ref[pl.ds(base, 8), :]
-            yrows = yi_ref[pl.ds(base, 8), :]
+            base = pl.multiple_of(step * 2 * gsteps, 8)
+            xrows = xi_ref[pl.ds(base, 2 * gsteps), :]
+            yrows = yi_ref[pl.ds(base, 2 * gsteps), :]
             sums = list(carry)
-            for s in range(4):
+            for s in range(gsteps):
                 hot_y = jnp.concatenate(
-                    [ones_where(box_row == yrows[2 * s + h : 2 * s + h + 1, :]) for h in range(2)], 1
+                    [ones_where(pack_lane == yrows[2 * s + h : 2 * s + h + 1, :]) for h in range(2)], 1
                 )
                 taken = dot(grid_ref[...], hot_y)
                 halves, swapped = [], []
                 for h in range(2):
-                    mask = box_row == xrows[2 * s + h : 2 * s + h + 1, :]
+                    mask = pack_row == xrows[2 * s + h : 2 * s + h + 1, :]
                     rows = []
                     for ch in range(nch):
-                        part = taken[ch * BOX : (ch + 1) * BOX, h * LANES : (h + 1) * LANES]
+                        part = taken[ch * PACK : (ch + 1) * PACK, h * LANES : (h + 1) * LANES]
                         row = jnp.sum(jnp.where(mask, part, 0.0), 0, keepdims=True)
                         rows.append(row)
                     halves.append(jnp.concatenate(rows + [blank], 0))
@@ -353,17 +417,18 @@
                     swapped.append(jnp.concatenate(other + [blank], 0))
                 ret = jnp.concatenate(halves, 0)
                 cross = jnp.concatenate(swapped, 0)
-                ret_ref[step * 4 + s] = ret
+                ret_ref[step * gsteps + s] = ret
                 for m in range(bands):
-                    other = zall_ref[m, step * 4 + s].astype(f32)
+                    other = zall_ref[m, step * gsteps + s].astype(f32)
                     sums[m] = sums[m] + other * ret
                     sums[bands + m] = sums[bands + m] + other * cross
             return tuple(sums)
 
         zero = jnp.zeros((16, LANES), f32)
-        sums = lax.fori_loop(0, count // 4, take_columns, (zero,) * (2 * bands))
-        radius = radius_rows(p_ref, cm_ref, grid_x, grid_y, grid_z)
-        band = p_ref[1]
+        sums = lax.fori_loop(0, count // gsteps, take_columns, (zero,) * (2 * bands))
+        radius = radius_rows(p, cm_ref, grid_x, grid_y, grid_z)
+        band = lax.axis_index("band")
+        oall_ref = oall()
         kin = [jnp.zeros((1, LANES), f32) for _ in range(2 * bands)]
         for h in range(2):
             lanes = slice(h * LANES, (h + 1) * LANES)
@@ -387,8 +452,9 @@
         carried = jnp.where(sub == nch, jnp.broadcast_to(row, (16, LANES)), 0.0)
         out_ref[...] = (ret_ref[...] + carried[None]).astype(bf16)
 
-    def finish(p_ref, cm_ref, orb_ref, rr_ref, tab_ref, applied_ref, sub_ref):
-        radius = radius_rows(p_ref, cm_ref, grid_x, grid_y, grid_z)
+    def finish(cm_ref, orb_ref, rr_ref, tab_ref, applied_ref, sub_ref):
+        p = lax.axis_index("pw")
+        radius = radius_rows(p, cm_ref, grid_x, grid_y, grid_z)
         got = rr_ref[...].astype(f32)
         right = jnp.concatenate(
             [got[:, h * 8 : (h + 1) * 8].reshape(count * 8, LANES) for h in range(2)], 1
@@ -403,23 +469,52 @@
         summed = summed + (
             pltpu.roll(summed, LANES - 2 * bands, 1) + pltpu.roll(summed, LANES - 4 * bands, 1)
         )
-        sub_ref[...] = summed * (1.0 / (grid_z * count * 2 * LANES))
+        summed = summed[nch : nch + 1] * (1.0 / (grid_z * count * 2 * LANES))
+        sub_ref[0] = summed[:, 0:bands]
+        sub_ref[1] = pltpu.roll(summed, LANES - bands, 1)[:, 0:bands]
 
     return to_columns, forward, backward, finish
 
 
-def call(kernel, out_shape, n_scalar, n_in, scratch=()):
-    smem = pl.BlockSpec(memory_space=pltpu.SMEM)
+class Late:
+    def __init__(self, source, target, semaphore):
+        self.copy = pltpu.make_async_copy(source, target, semaphore)
+        self.target = target
+        self.waiting = True
+        self.copy.start()
+
+    def __call__(self):
+        if self.waiting:
+            self.copy.wait()
+            self.waiting = False
+        return self.target
+
+
+def call(kernel, out_shape, operands, scratch=(), late=(), mib=VMEM_MIB):
     vmem = pl.BlockSpec(memory_space=pltpu.VMEM)
+    hbm = pl.BlockSpec(memory_space=pltpu.HBM)
     multiple = isinstance(out_shape, (list, tuple))
+    n_in, n_out, n_own = len(operands), len(out_shape) if multiple else 1, len(scratch)
+
+    def body(*refs):
+        given, rest = list(refs[:n_in]), refs[n_in : n_in + n_out + n_own]
+        if late:
+            buffers, semaphores = refs[n_in + n_out + n_own : -1], refs[-1]
+            for k, at in enumerate(late):
+                given[at] = Late(given[at], buffers[k], semaphores.at[k])
+        kernel(*given, *rest)
+
+    extra = [pltpu.VMEM(operands[at].shape, operands[at].dtype) for at in late]
+    if late:
+        extra.append(pltpu.SemaphoreType.DMA((len(late),)))
     return pl.pallas_call(
-        kernel,
+        body,
         out_shape=out_shape,
-        in_specs=[smem] * n_scalar + [vmem] * n_in,
-        out_specs=[vmem] * len(out_shape) if multiple else vmem,
-        scratch_shapes=list(scratch),
-        compiler_params=pltpu.CompilerParams(vmem_limit_bytes=56 * 1024 * 1024),
-    )
+        in_specs=[hbm if at in late else vmem for at in range(n_in)],
+        out_specs=[vmem] * n_out if multiple else vmem,
+        scratch_shapes=list(scratch) + extra,
+        compiler_params=pltpu.CompilerParams(vmem_limit_bytes=mib * 1024 * 1024),
+    )(*operands)
 
 
 def per_device(orbitals, column_map, potential, projectors, block_index, block_atom, coupling):
@@ -430,47 +525,51 @@
     count, bands = lax.axis_size("pw"), lax.axis_size("band")
     ncolumns = column_map.shape[0]
     half = box_half(grid_x, grid_y, ncolumns)
-    zf, zb, yf, xf, xb, yb = make_tables(grid_z, grid_x, grid_y, z_local, half)
+    zf, zb, yf, yft, xf, xb, yb, ybt = make_tables(grid_z, grid_x, grid_y, z_local, half)
     sizes = (grid_z, grid_x, grid_y, z_local, count, bands, natoms, nproj, entries, half)
     to_columns, forward, backward, finish = build(sizes)
     shape = jax.ShapeDtypeStruct
     blocks = z_local * grid_x * grid_y // BLOCK
     cj = 2 * nproj
 
-    place = jnp.stack([lax.axis_index("pw"), lax.axis_index("band")]).astype(i32)
     cm = column_map.reshape(ncolumns // LANES, LANES)
     orb = orbitals.reshape(2 * grid_z, col_local)
     bi = block_index.reshape(entries // LANES, LANES)
     at = block_atom.reshape(entries // LANES, LANES)
     coup = coupling.reshape(natoms, nproj * nproj).T
+    proj = projectors.reshape(entries * nproj, BLOCK)
     packet = (count, 16, LANES)
 
-    sent = call(to_columns, shape(packet, bf16), 1, 3)(place, cm, orb, zf)
+    sent = call(to_columns, shape(packet, bf16), (cm, orb, zf), late=(0, 1, 2), mib=ALL_MIB)
     planes = lax.all_to_all(sent, "pw", split_axis=0, concat_axis=0, tiled=True)
     index_scratch = [pltpu.VMEM(cm.shape, i32), pltpu.VMEM(cm.shape, i32)]
     pf_scratch = pltpu.VMEM((entries * nproj, BLOCK), f32)
-    real_space, window, to_send = call(
+    real_space, window, to_send, near = call(
         forward,
-        (shape((blocks, 2 * BLOCK), bf16), shape((cj, SLOTS), f32), shape((count, cj, LANES), f32)),
-        1, 7,
-        index_scratch + [pltpu.VMEM((2 * z_local * BOX, BOX), f32), pf_scratch],
-    )(place, cm, planes, yf, xf, bi, at, projectors)
+        (shape((blocks, 2 * BLOCK), bf16), shape((cj, SLOTS), f32), shape((count, cj, LANES), f32),
+         shape((nproj * nproj, SLOTS), f32)),
+        (cm, planes, yf, yft, xf, bi, at, proj, coup),
+        index_scratch + [pltpu.VMEM((2 * z_local * PACK, 256), f32), pf_scratch],
+        late=(0, 2, 3, 4, 8, 5, 7, 6),
+    )
     other = lax.all_to_all(to_send, "pw", split_axis=0, concat_axis=0, tiled=True)
     all_planes = lax.all_gather(planes, "band", axis=0, tiled=False)
     all_orb = lax.all_gather(orb, "band", axis=0, tiled=False)
     back = call(
-        backward, shape(packet, bf16), 1, 13,
+        backward, shape(packet, bf16),
+        (cm, other, window, real_space, potential, near, bi, at, proj, xb, yb, ybt, all_planes, all_orb),
         index_scratch
-        + [pf_scratch, pltpu.VMEM((2 * z_local * BOX, BOX), bf16), pltpu.VMEM(packet, f32)]
+        + [pf_scratch, pltpu.VMEM((2 * z_local * PACK, 256), bf16), pltpu.VMEM(packet, f32)]
         + [pltpu.VMEM((z_local * grid_x, LANES), f32)] * 2,
-    )(place, cm, other, window, real_space, potential, coup, bi, at, projectors, xb, yb, all_planes, all_orb)
+        late=(7, 8, 6, 4, 9, 10, 11, 0, 12, 13),
+    )
     returned = lax.all_to_all(back, "pw", split_axis=0, concat_axis=0, tiled=True)
     applied, sums = call(
-        finish, (shape((2 * grid_z, col_local), f32), shape((8, LANES), f32)), 1, 4
-    )(place, cm, orb, returned, zb)
+        finish, (shape((2 * grid_z, col_local), f32), shape((2, 1, bands), f32)),
+        (cm, orb, returned, zb),
+    )
     applied = applied.reshape(1, 2, grid_z, col_local)
-    subspace = sums[2 * z_local, : 2 * bands].reshape(2, bands, 1)
-    return applied, subspace
+    return applied, sums.transpose(0, 2, 1)
 
 
 def solution(mesh):

time: 134 us -> 120 us (0.90)
  Pallas kernels: 43.1 us -> 30.8 us
    pallas_call x4, Pallas kernels: 43.1 us -> 30.8 us  [call(): pl.pallas_call(body, out_shape=out_shape, in_specs=[hbm if at in late els...]
  transfers between devices with their start and end apart: 2 -> 2, of which waited for: 1 -> 1; matrix products, arithmetic and copies ran while one was open for 0% -> 0% of each run, Pallas kernels for 13% -> 10%
where the time goes in v1:
time: 120 us
  blocking collectives  62.1 us (52%)
  Pallas kernels  30.8 us (26%)
  between operations  14.2 us (12%)
  starting transfers between devices  5.9 us (5%)
  waiting for transfers between devices  5.64 us (5%)
    pallas_call x4, Pallas kernels, call(): pl.pallas_call(body, out_shape=out_shape, in_specs=[hbm if at in late els...  30.8 us
    all_to_all x1, blocking collectives, per_device(): planes = lax.all_to_all(sent, 'pw', split_axis=0, concat_axis=0, tiled=True)  28.5 us
    all_to_all x1, blocking collectives, per_device(): lax.all_to_all(back, 'pw', split_axis=0, concat_axis=0, tiled=True)  21.2 us
    all_gather x1, blocking collectives, per_device(): all_orb = lax.all_gather(orb, 'band', axis=0, tiled=False)  12.4 us
    all_to_all x1, starting transfers between devices, per_device(): lax.all_to_all(to_send, 'pw', split_axis=0, concat_axis=0, tiled=True)  5.87 us
    all_to_all x1, waiting for transfers between devices, per_device(): lax.all_to_all(to_send, 'pw', split_axis=0, concat_axis=0, tiled=True)  5.62 us
  transfers between devices with their start and end apart: 2, of which 1 were waited for; matrix products, arithmetic and copies ran while one was open for 0% of the time, Pallas kernels for 10%

profile of v1, /device:TPU:6, one launch (start us, length us, event | category | flops | bytes accessed | tf_op | source)
XLA Modules:
  0.0 119.7 jit_solution(17287039317275405771)
XLA Ops:
  7.2 0.0 all-gather.3.cloned.1.call-start
  7.2 0.0 copy-start.6
  7.2 2.2 %shard_map.158 = bf16[64,16,128]{2,1,0:T(8,128)(2,1)} custom-call(s32[128,128]{1,0:T(8,128)} %bitcast.17, bf16[384,256]{1,0:T(8,128)(2,1)} %bitcast.14, bf16[512,384]{1,0:T(8,128)(2,1)} %constant.16.clone.refs_2_), custom_call_target="tpu_custom_call" | custom-call | tf_op jit(solution)/shard_map/pallas_call | solution.py:510
  9.4 0.0 copy-start.2
  9.4 0.0 copy-start.4
  9.4 0.0 copy-start.9
  9.4 28.5 %all_to_all.15.refs_1_ = bf16[64,16,128]{2,1,0:T(8,128)(2,1)} all-to-all(bf16[64,16,128]{2,1,0:T(8,128)(2,1)} %shard_map.158), channel_id=1, replica_groups=mesh['band'=4,'pw'=64] {'pw'}, dimensions={0} | all-to-all | bytes 524288 | tf_op jit(solution)/shard_map/all_to_all | solution.py:544
  38.0 0.0 all-gather.3.cloned.1.call-update
  38.0 0.0 copy-start.11
  38.0 0.0 copy-start.10
  38.1 0.9 copy-done
  39.0 12.4 %shard_map.159 = (bf16[864,256]{1,0:T(8,128)(2,1)S(1)}, f32[16,256]{1,0:T(8,128)S(1)}, f32[64,16,128]{2,1,0:T(8,128)}, f32[64,256]{1,0:T(8,128)S(1)}) custom-call(s32[128,128]{1,0:T(8,128)S(1)} %bitcast.18, bf16[64,16,128]{2,1,0:T(8,128)(2,1)S(1)} %copy-done, bf16[256,512]{1,0:T(8,128)(2,1)S(1)} %copy-done.6, bf16[64,512]{1,0:T(8,128)(2,1)S(1)} %copy-done.9, ...), custom_call_target="tpu_custom_call" | custom-call | tf_op jit(solution)/shard_map/pallas_call | solution.py:510
  51.4 0.0 copy-start.1
  51.4 5.9 %all-to-all-start.1 = ((f32[64,16,128]{2,1,0:T(8,128)}), f32[64,16,128]{2,1,0:T(8,128)S(1)}, u32[]{:S(2)}, u32[]{:S(2)}) async-start(f32[64,16,128]{2,1,0:T(8,128)} %get-tuple-element.8), calls=%async_computation.1 | async-start | bytes 1048576 | tf_op jit(solution)/shard_map/all_to_all | solution.py:555
  57.3 0.0 copy-start.5
  57.3 0.0 copy-start.7
  57.3 0.0 copy-start.8
  57.3 12.4 %all_gather.11.refs_13_ = bf16[4,384,256]{2,1,0:T(8,128)(2,1)} all-gather(bf16[1,384,256]{2,1,0:T(8,128)(2,1)S(1)} %bitcast.15), channel_id=1, replica_groups=mesh['band'=4,'pw'=64] {'band'}, dimensions={0}, use_global_device_ids=true | all-gather | bytes 983040 | tf_op jit(solution)/shard_map/all_gather | solution.py:557
  69.7 5.6 %all-to-all-done.1.refs_1_ = f32[64,16,128]{2,1,0:T(8,128)S(1)} async-done(((f32[64,16,128]{2,1,0:T(8,128)}), f32[64,16,128]{2,1,0:T(8,128)S(1)}, u32[]{:S(2)}, u32[]{:S(2)}) %all-to-all-start.1) | async-done | bytes 524320 | tf_op jit(solution)/shard_map/all_to_all | solution.py:555
  75.4 0.0 copy-done.8
  75.4 15.2 %shard_map.160 = bf16[64,16,128]{2,1,0:T(8,128)(2,1)S(1)} custom-call(s32[128,128]{1,0:T(8,128)S(1)} %bitcast.19, f32[64,16,128]{2,1,0:T(8,128)S(1)} %all-to-all-done.1.refs_1_, f32[16,256]{1,0:T(8,128)S(1)} %get-tuple-element.9.refs_2_, bf16[864,256]{1,0:T(8,128)(2,1)S(1)} %get-tuple-element.10.refs_3_, f32[3,192,192]{2,1,0:T(8,128)} %refs_4_.2, ...), custom_call_target="tpu_custom_call" | custom-call | tf_op jit(solution)/shard_map/pallas_call | solution.py:510
  90.6 0.0 copy-start.3
  90.6 21.2 %all_to_all.16.refs_2_ = bf16[64,16,128]{2,1,0:T(8,128)(2,1)S(1)} all-to-all(bf16[64,16,128]{2,1,0:T(8,128)(2,1)S(1)} %shard_map.160), channel_id=1, replica_groups=mesh['band'=4,'pw'=64] {'pw'}, dimensions={0} | all-to-all | bytes 524288 | tf_op jit(solution)/shard_map/all_to_all | solution.py:566
  111.8 1.0 shard_map.161
  (12 shorter events, 0.0 us)
Async XLA Ops:
  7.2 68.2 %all-gather.3.cloned.1.call-start = ((), (), s32[]{:S(2)}) async-start(), calls=%async_computation.3 | async-start | bytes 1310720 | tf_op jit(solution)/shard_map/all_gather | solution.py:556
  7.2 30.8 %copy-start.6 = (bf16[256,512]{1,0:T(8,128)(2,1)S(1)}, bf16[256,512]{1,0:T(8,128)(2,1)}, u32[]{:S(2)}) copy-start(bf16[256,512]{1,0:T(8,128)(2,1)} %constant.18.clone.refs_2_) | copy-start | bytes 786436
  9.4 28.6 %copy-start.2 = (s32[16384]{0:T(1024)S(1)}, s32[16384]{0:T(1024)}, u32[]{:S(2)}) copy-start(s32[16384]{0:T(1024)} %param.16) | copy-start | bytes 196612
  9.4 28.6 %copy-start.4 = (bf16[384,320]{1,0:T(8,128)(2,1)S(1)}, bf16[384,320]{1,0:T(8,128)(2,1)}, u32[]{:S(2)}) copy-start(bf16[384,320]{1,0:T(8,128)(2,1)} %constant.20.clone.refs_4_) | copy-start | bytes 737284
  9.4 28.6 %copy-start.9 = (bf16[64,512]{1,0:T(8,128)(2,1)S(1)}, bf16[64,512]{1,0:T(8,128)(2,1)}, u32[]{:S(2)}) copy-start(bf16[64,512]{1,0:T(8,128)(2,1)} %constant.19.clone.refs_3_) | copy-start | bytes 196612
  38.0 1.0 copy-start
  38.0 0.9 copy-start.11
  38.0 0.9 copy-start.10
  51.4 5.9 %copy-start.1 = (bf16[1,2,192,256]{3,2,1,0:T(8,128)(2,1)S(1)}, bf16[1,2,192,256]{3,2,1,0:T(8,128)(2,1)}, u32[]{:S(2)}) copy-start(bf16[1,2,192,256]{3,2,1,0:T(8,128)(2,1)} %param.15) | copy-start | bytes 589828
  51.4 24.0 %all-to-all-start.1 = ((f32[64,16,128]{2,1,0:T(8,128)}), f32[64,16,128]{2,1,0:T(8,128)S(1)}, u32[]{:S(2)}, u32[]{:S(2)}) async-start(f32[64,16,128]{2,1,0:T(8,128)} %get-tuple-element.8), calls=%async_computation.1 | async-start | bytes 1048576 | tf_op jit(solution)/shard_map/all_to_all | solution.py:555
  57.3 18.1 %copy-start.5 = (bf16[2,256,256]{2,1,0:T(8,128)(2,1)S(1)}, bf16[2,256,256]{2,1,0:T(8,128)(2,1)}, u32[]{:S(2)}) copy-start(bf16[2,256,256]{2,1,0:T(8,128)(2,1)} %constant.22.clone.refs_10_) | copy-start | bytes 786436
  57.3 18.1 %copy-start.7 = (bf16[320,384]{1,0:T(8,128)(2,1)S(1)}, bf16[320,384]{1,0:T(8,128)(2,1)}, u32[]{:S(2)}) copy-start(bf16[320,384]{1,0:T(8,128)(2,1)} %constant.21.clone.refs_9_) | copy-start | bytes 737284
  57.3 18.1 %copy-start.8 = (bf16[2,64,256]{2,1,0:T(8,128)(2,1)S(1)}, bf16[2,64,256]{2,1,0:T(8,128)(2,1)}, u32[]{:S(2)}) copy-start(bf16[2,64,256]{2,1,0:T(8,128)(2,1)} %constant.23.clone.refs_11_) | copy-start | bytes 196612
  90.6 21.2 %copy-start.3 = (bf16[384,512]{1,0:T(8,128)(2,1)S(1)}, bf16[384,512]{1,0:T(8,128)(2,1)}, u32[]{:S(2)}) copy-start(bf16[384,512]{1,0:T(8,128)(2,1)} %constant.17.clone.refs_3_) | copy-start | bytes 1179652
Sparse Core Ops, SparseCore 0:
  38.1 17.3 all-gather.2

commit v2 on v1

--- a/solution.py
+++ b/solution.py
@@ -132,8 +132,8 @@
     chunks = entries // LANES
     cj = 2 * nproj
     nch = 2 * z_local
-    steps = 16
-    gsteps = 8
+    steps = 32
+    gsteps = 32
     rows_c = z_local * PACK
 
     def block_rows(values):
@@ -406,12 +406,15 @@
                 taken = dot(grid_ref[...], hot_y)
                 halves, swapped = [], []
                 for h in range(2):
-                    mask = pack_row == xrows[2 * s + h : 2 * s + h + 1, :]
+                    mask = ones_where(pack_row == xrows[2 * s + h : 2 * s + h + 1, :])
                     rows = []
                     for ch in range(nch):
                         part = taken[ch * PACK : (ch + 1) * PACK, h * LANES : (h + 1) * LANES]
-                        row = jnp.sum(jnp.where(mask, part, 0.0), 0, keepdims=True)
-                        rows.append(row)
+                        part = (part.astype(bf16) * mask).reshape(PACK // 16, 16, LANES)
+                        own = part[0]
+                        for k in range(1, PACK // 16):
+                            own = own + part[k]
+                        rows.append(jnp.sum(own.astype(f32), 0, keepdims=True))
                     halves.append(jnp.concatenate(rows + [blank], 0))
                     other = rows[z_local:] + [-r for r in rows[:z_local]]
                     swapped.append(jnp.concatenate(other + [blank], 0))
@@ -561,7 +564,7 @@
         index_scratch
         + [pf_scratch, pltpu.VMEM((2 * z_local * PACK, 256), bf16), pltpu.VMEM(packet, f32)]
         + [pltpu.VMEM((z_local * grid_x, LANES), f32)] * 2,
-        late=(7, 8, 6, 4, 9, 10, 11, 0, 12, 13),
+        late=(7, 8, 6, 4, 9, 10, 11, 0, 12, 13), mib=50,
     )
     returned = lax.all_to_all(back, "pw", split_axis=0, concat_axis=0, tiled=True)
     applied, sums = call(

time: 120 us -> 118 us (0.983)
  Pallas kernels: 30.8 us -> 28.9 us
    pallas_call x4, Pallas kernels: 30.8 us -> 28.9 us  [call(): pl.pallas_call(body, out_shape=out_shape, in_specs=[hbm if at in late els...]
where the time goes in v2:
time: 118 us; the launch traced here: 117 us
  blocking collectives  61.3 us (52%)
  Pallas kernels  28.9 us (24%)
  between operations  14.2 us (12%)
  waiting for transfers between devices  6.07 us (5%)
  starting transfers between devices  5.92 us (5%)
    pallas_call x4, Pallas kernels, call(): pl.pallas_call(body, out_shape=out_shape, in_specs=[hbm if at in late els...  28.9 us
    all_to_all x1, blocking collectives, per_device(): planes = lax.all_to_all(sent, 'pw', split_axis=0, concat_axis=0, tiled=True)  28.5 us
    all_to_all x1, blocking collectives, per_device(): lax.all_to_all(back, 'pw', split_axis=0, concat_axis=0, tiled=True)  20.8 us
    all_gather x1, blocking collectives, per_device(): all_orb = lax.all_gather(orb, 'band', axis=0, tiled=False)  12 us
    all_to_all x1, waiting for transfers between devices, per_device(): lax.all_to_all(to_send, 'pw', split_axis=0, concat_axis=0, tiled=True)  6.05 us
    all_to_all x1, starting transfers between devices, per_device(): lax.all_to_all(to_send, 'pw', split_axis=0, concat_axis=0, tiled=True)  5.88 us
  transfers between devices with their start and end apart: 2, of which 1 were waited for; matrix products, arithmetic and copies ran while one was open for 0% of the time, Pallas kernels for 10%

profile of v2, /device:TPU:6, one launch (start us, length us, event | category | flops | bytes accessed | tf_op | source)
XLA Modules:
  0.0 117.3 jit_solution(6727524541421308035)
XLA Ops:
  7.2 0.0 all-gather.3.cloned.1.call-start
  7.2 0.0 copy-start.7
  7.2 2.2 %shard_map.158 = bf16[64,16,128]{2,1,0:T(8,128)(2,1)} custom-call(s32[128,128]{1,0:T(8,128)} %bitcast.17, bf16[384,256]{1,0:T(8,128)(2,1)} %bitcast.14, bf16[512,384]{1,0:T(8,128)(2,1)} %constant.16.clone.refs_2_), custom_call_target="tpu_custom_call" | custom-call | tf_op jit(solution)/shard_map/pallas_call | solution.py:513
  9.4 0.0 copy-start.2
  9.4 0.0 copy-start.5
  9.4 0.0 copy-start.10
  9.4 28.5 %all_to_all.15.refs_1_ = bf16[64,16,128]{2,1,0:T(8,128)(2,1)} all-to-all(bf16[64,16,128]{2,1,0:T(8,128)(2,1)} %shard_map.158), channel_id=1, replica_groups=mesh['band'=4,'pw'=64] {'pw'}, dimensions={0} | all-to-all | bytes 524288 | tf_op jit(solution)/shard_map/all_to_all | solution.py:547
  38.0 0.0 all-gather.3.cloned.1.call-update
  38.0 0.0 copy-start.12
  38.0 0.0 copy-start.11
  38.1 0.9 copy-done
  39.0 12.0 %shard_map.159 = (bf16[864,256]{1,0:T(8,128)(2,1)S(1)}, f32[16,256]{1,0:T(8,128)S(1)}, f32[64,16,128]{2,1,0:T(8,128)}, f32[64,256]{1,0:T(8,128)S(1)}) custom-call(s32[128,128]{1,0:T(8,128)S(1)} %bitcast.18, bf16[64,16,128]{2,1,0:T(8,128)(2,1)S(1)} %copy-done, bf16[256,512]{1,0:T(8,128)(2,1)S(1)} %copy-done.7, bf16[64,512]{1,0:T(8,128)(2,1)S(1)} %copy-done.10, ...), custom_call_target="tpu_custom_call" | custom-call | tf_op jit(solution)/shard_map/pallas_call | solution.py:513
  51.0 0.0 copy-start.1
  51.0 0.0 copy-start.8
  51.0 5.9 %all-to-all-start.1 = ((f32[64,16,128]{2,1,0:T(8,128)}), f32[64,16,128]{2,1,0:T(8,128)S(1)}, u32[]{:S(2)}, u32[]{:S(2)}) async-start(f32[64,16,128]{2,1,0:T(8,128)} %get-tuple-element.8), calls=%async_computation.1 | async-start | bytes 1048576 | tf_op jit(solution)/shard_map/all_to_all | solution.py:558
  56.9 0.0 copy-start.3
  56.9 0.0 copy-start.6
  56.9 0.0 copy-start.9
  57.0 12.0 %all_gather.11.refs_13_ = bf16[4,384,256]{2,1,0:T(8,128)(2,1)S(1)} all-gather(bf16[1,384,256]{2,1,0:T(8,128)(2,1)S(1)} %bitcast.15), channel_id=1, replica_groups=mesh['band'=4,'pw'=64] {'band'}, dimensions={0}, use_global_device_ids=true | all-gather | bytes 983040 | tf_op jit(solution)/shard_map/all_gather | solution.py:560
  68.9 6.1 %all-to-all-done.1.refs_1_ = f32[64,16,128]{2,1,0:T(8,128)S(1)} async-done(((f32[64,16,128]{2,1,0:T(8,128)}), f32[64,16,128]{2,1,0:T(8,128)S(1)}, u32[]{:S(2)}, u32[]{:S(2)}) %all-to-all-start.1) | async-done | bytes 524320 | tf_op jit(solution)/shard_map/all_to_all | solution.py:558
  75.0 13.6 %shard_map.160 = bf16[64,16,128]{2,1,0:T(8,128)(2,1)S(1)} custom-call(s32[128,128]{1,0:T(8,128)S(1)} %bitcast.19, f32[64,16,128]{2,1,0:T(8,128)S(1)} %all-to-all-done.1.refs_1_, f32[16,256]{1,0:T(8,128)S(1)} %get-tuple-element.9.refs_2_, bf16[864,256]{1,0:T(8,128)(2,1)S(1)} %get-tuple-element.10.refs_3_, f32[3,192,192]{2,1,0:T(8,128)S(1)} %copy-done.3, ...), custom_call_target="tpu_custom_call" | custom-call | tf_op jit(solution)/shard_map/pallas_call | solution.py:513
  88.6 0.0 copy-start.4
  88.6 20.8 %all_to_all.16.refs_2_ = bf16[64,16,128]{2,1,0:T(8,128)(2,1)S(1)} all-to-all(bf16[64,16,128]{2,1,0:T(8,128)(2,1)S(1)} %shard_map.160), channel_id=1, replica_groups=mesh['band'=4,'pw'=64] {'pw'}, dimensions={0} | all-to-all | bytes 524288 | tf_op jit(solution)/shard_map/all_to_all | solution.py:569
  109.4 1.0 shard_map.161
  (14 shorter events, 0.0 us)
Async XLA Ops:
  7.2 67.8 %all-gather.3.cloned.1.call-start = ((), (), s32[]{:S(2)}) async-start(), calls=%async_computation.3 | async-start | bytes 1310720 | tf_op jit(solution)/shard_map/all_gather | solution.py:559
  7.2 30.8 %copy-start.7 = (bf16[256,512]{1,0:T(8,128)(2,1)S(1)}, bf16[256,512]{1,0:T(8,128)(2,1)}, u32[]{:S(2)}) copy-start(bf16[256,512]{1,0:T(8,128)(2,1)} %constant.18.clone.refs_2_) | copy-start | bytes 786436
  9.4 28.6 %copy-start.2 = (s32[16384]{0:T(1024)S(1)}, s32[16384]{0:T(1024)}, u32[]{:S(2)}) copy-start(s32[16384]{0:T(1024)} %param.16) | copy-start | bytes 196612
  9.4 28.6 %copy-start.5 = (bf16[384,320]{1,0:T(8,128)(2,1)S(1)}, bf16[384,320]{1,0:T(8,128)(2,1)}, u32[]{:S(2)}) copy-start(bf16[384,320]{1,0:T(8,128)(2,1)} %constant.20.clone.refs_4_) | copy-start | bytes 737284
  9.4 28.6 %copy-start.10 = (bf16[64,512]{1,0:T(8,128)(2,1)S(1)}, bf16[64,512]{1,0:T(8,128)(2,1)}, u32[]{:S(2)}) copy-start(bf16[64,512]{1,0:T(8,128)(2,1)} %constant.19.clone.refs_3_) | copy-start | bytes 196612
  38.0 1.0 copy-start
  38.0 0.9 copy-start.12
  38.0 0.9 copy-start.11
  51.0 5.9 %copy-start.1 = (bf16[1,2,192,256]{3,2,1,0:T(8,128)(2,1)S(1)}, bf16[1,2,192,256]{3,2,1,0:T(8,128)(2,1)}, u32[]{:S(2)}) copy-start(bf16[1,2,192,256]{3,2,1,0:T(8,128)(2,1)} %param.15) | copy-start | bytes 589828
  51.0 24.0 %copy-start.8 = (bf16[320,384]{1,0:T(8,128)(2,1)S(1)}, bf16[320,384]{1,0:T(8,128)(2,1)}, u32[]{:S(2)}) copy-start(bf16[320,384]{1,0:T(8,128)(2,1)} %constant.21.clone.refs_9_) | copy-start | bytes 737284
  51.0 23.9 %all-to-all-start.1 = ((f32[64,16,128]{2,1,0:T(8,128)}), f32[64,16,128]{2,1,0:T(8,128)S(1)}, u32[]{:S(2)}, u32[]{:S(2)}) async-start(f32[64,16,128]{2,1,0:T(8,128)} %get-tuple-element.8), calls=%async_computation.1 | async-start | bytes 1048576 | tf_op jit(solution)/shard_map/all_to_all | solution.py:558
  56.9 18.1 %copy-start.3 = (f32[3,192,192]{2,1,0:T(8,128)S(1)}, f32[3,192,192]{2,1,0:T(8,128)}, u32[]{:S(2)}) copy-start(f32[3,192,192]{2,1,0:T(8,128)} %refs_4_.2) | copy-start | bytes 1327108
  56.9 18.0 %copy-start.6 = (bf16[2,256,256]{2,1,0:T(8,128)(2,1)S(1)}, bf16[2,256,256]{2,1,0:T(8,128)(2,1)}, u32[]{:S(2)}) copy-start(bf16[2,256,256]{2,1,0:T(8,128)(2,1)} %constant.22.clone.refs_10_) | copy-start | bytes 786436
  56.9 18.0 %copy-start.9 = (bf16[2,64,256]{2,1,0:T(8,128)(2,1)S(1)}, bf16[2,64,256]{2,1,0:T(8,128)(2,1)}, u32[]{:S(2)}) copy-start(bf16[2,64,256]{2,1,0:T(8,128)(2,1)} %constant.23.clone.refs_11_) | copy-start | bytes 196612
  88.6 20.8 %copy-start.4 = (bf16[384,512]{1,0:T(8,128)(2,1)S(1)}, bf16[384,512]{1,0:T(8,128)(2,1)}, u32[]{:S(2)}) copy-start(bf16[384,512]{1,0:T(8,128)(2,1)} %constant.17.clone.refs_3_) | copy-start | bytes 1179652
Sparse Core Ops, SparseCore 0:
  38.1 17.4 all-gather.2

commit v3 on v2

--- a/solution.py
+++ b/solution.py
@@ -176,6 +176,11 @@
         square = nproj * nproj
         return near[0:square] + near[square : 2 * square] + near[2 * square : 3 * square]
 
+    def hot_rows(numbers, row, count):
+        wide = jnp.broadcast_to(row.astype(f32), (16, LANES)).astype(bf16)
+        same = numbers.reshape(count // 16, 16, LANES) == wide[None]
+        return jnp.where(same, jnp.ones((), bf16), jnp.zeros((), bf16))
+
     def to_columns(cm, orb, table, out_ref):
         p = lax.axis_index("pw")
         radius = radius_rows(p, cm(), grid_x, grid_y, grid_z)
@@ -193,8 +198,8 @@
         p = lax.axis_index("pw")
         box_indices(cm(), xi_ref, yi_ref)
         acc_ref[...] = jnp.zeros_like(acc_ref)
-        pack_row = iota((PACK, LANES), 0)
-        pack_lane = iota((256, LANES), 0)
+        pack_row = iota((PACK, LANES), 0).astype(f32).astype(bf16)
+        pack_lane = iota((256, LANES), 0).astype(f32).astype(bf16)
 
         def add_columns(step, carry):
             xrows = xi_ref[pl.ds(pl.multiple_of(step * 2 * steps, 8), 2 * steps), :]
@@ -204,8 +209,8 @@
                 v = zr_ref[step * steps + s].astype(f32)
                 for h in range(2):
                     r = 2 * s + h
-                    hot = ones_where(pack_row == xrows[r : r + 1, :]).reshape(PACK // 16, 16, LANES)
-                    right.append(ones_where(pack_lane == yrows[r : r + 1, :]))
+                    hot = hot_rows(pack_row, xrows[r : r + 1, :], PACK)
+                    right.append(hot_rows(pack_lane, yrows[r : r + 1, :], 256).reshape(256, LANES))
                     rows = []
                     for ch in range(nch):
                         one = v[h * 8 + ch : h * 8 + ch + 1, :]
@@ -390,8 +395,8 @@
                     ].astype(bf16)
         cm_ref, zall_ref = cm(), zall()
         box_indices(cm_ref, xi_ref, yi_ref)
-        pack_row = iota((PACK, LANES), 0)
-        pack_lane = iota((256, LANES), 0)
+        pack_row = iota((PACK, LANES), 0).astype(f32).astype(bf16)
+        pack_lane = iota((256, LANES), 0).astype(f32).astype(bf16)
         blank = jnp.zeros((8 - nch, LANES), f32)
 
         def take_columns(step, carry):
@@ -401,12 +406,12 @@
             sums = list(carry)
             for s in range(gsteps):
                 hot_y = jnp.concatenate(
-                    [ones_where(pack_lane == yrows[2 * s + h : 2 * s + h + 1, :]) for h in range(2)], 1
+                    [hot_rows(pack_lane, yrows[2 * s + h : 2 * s + h + 1, :], 256).reshape(256, LANES) for h in range(2)], 1
                 )
                 taken = dot(grid_ref[...], hot_y)
                 halves, swapped = [], []
                 for h in range(2):
-                    mask = ones_where(pack_row == xrows[2 * s + h : 2 * s + h + 1, :])
+                    mask = hot_rows(pack_row, xrows[2 * s + h : 2 * s + h + 1, :], PACK).reshape(PACK, LANES)
                     rows = []
                     for ch in range(nch):
                         part = taken[ch * PACK : (ch + 1) * PACK, h * LANES : (h + 1) * LANES]

time: 118 us -> 117 us (level)
  no operation moved by 1% of the time
where the time goes in v3:
time: 117 us; the launch traced here: 116 us
  blocking collectives  61.3 us (52%)
  Pallas kernels  27.9 us (24%)
  between operations  14.2 us (12%)
  waiting for transfers between devices  6.08 us (5%)
  starting transfers between devices  5.91 us (5%)
    all_to_all x1, blocking collectives, per_device(): planes = lax.all_to_all(sent, 'pw', split_axis=0, concat_axis=0, tiled=True)  28.5 us
    pallas_call x4, Pallas kernels, call(): pl.pallas_call(body, out_shape=out_shape, in_specs=[hbm if at in late els...  27.9 us
    all_to_all x1, blocking collectives, per_device(): lax.all_to_all(back, 'pw', split_axis=0, concat_axis=0, tiled=True)  20.8 us
    all_gather x1, blocking collectives, per_device(): all_orb = lax.all_gather(orb, 'band', axis=0, tiled=False)  12 us
    all_to_all x1, waiting for transfers between devices, per_device(): lax.all_to_all(to_send, 'pw', split_axis=0, concat_axis=0, tiled=True)  6.06 us
    all_to_all x1, starting transfers between devices, per_device(): lax.all_to_all(to_send, 'pw', split_axis=0, concat_axis=0, tiled=True)  5.87 us
  transfers between devices with their start and end apart: 2, of which 1 were waited for; matrix products, arithmetic and copies ran while one was open for 0% of the time, Pallas kernels for 10%

profile of v3, /device:TPU:6, one launch (start us, length us, event | category | flops | bytes accessed | tf_op | source)
XLA Modules:
  0.0 116.3 jit_solution(16583012944398087485)
XLA Ops:
  7.2 0.0 all-gather.3.cloned.1.call-start
  7.2 0.0 copy-start.7
  7.2 2.2 %shard_map.158 = bf16[64,16,128]{2,1,0:T(8,128)(2,1)} custom-call(s32[128,128]{1,0:T(8,128)} %bitcast.17, bf16[384,256]{1,0:T(8,128)(2,1)} %bitcast.14, bf16[512,384]{1,0:T(8,128)(2,1)} %constant.16.clone.refs_2_), custom_call_target="tpu_custom_call" | custom-call | tf_op jit(solution)/shard_map/pallas_call | solution.py:518
  9.4 0.0 copy-start.2
  9.4 0.0 copy-start.5
  9.4 0.0 copy-start.10
  9.4 28.5 %all_to_all.15.refs_1_ = bf16[64,16,128]{2,1,0:T(8,128)(2,1)} all-to-all(bf16[64,16,128]{2,1,0:T(8,128)(2,1)} %shard_map.158), channel_id=1, replica_groups=mesh['band'=4,'pw'=64] {'pw'}, dimensions={0} | all-to-all | bytes 524288 | tf_op jit(solution)/shard_map/all_to_all | solution.py:552
  38.0 0.0 all-gather.3.cloned.1.call-update
  38.0 0.0 copy-start.12
  38.0 0.0 copy-start.11
  38.1 0.9 copy-done
  39.0 12.0 %shard_map.159 = (bf16[864,256]{1,0:T(8,128)(2,1)S(1)}, f32[16,256]{1,0:T(8,128)S(1)}, f32[64,16,128]{2,1,0:T(8,128)}, f32[64,256]{1,0:T(8,128)S(1)}) custom-call(s32[128,128]{1,0:T(8,128)S(1)} %bitcast.18, bf16[64,16,128]{2,1,0:T(8,128)(2,1)S(1)} %copy-done, bf16[256,512]{1,0:T(8,128)(2,1)S(1)} %copy-done.7, bf16[64,512]{1,0:T(8,128)(2,1)S(1)} %copy-done.10, ...), custom_call_target="tpu_custom_call" | custom-call | tf_op jit(solution)/shard_map/pallas_call | solution.py:518
  51.0 0.0 copy-start.1
  51.0 0.0 copy-start.8
  51.0 5.9 %all-to-all-start.1 = ((f32[64,16,128]{2,1,0:T(8,128)}), f32[64,16,128]{2,1,0:T(8,128)S(1)}, u32[]{:S(2)}, u32[]{:S(2)}) async-start(f32[64,16,128]{2,1,0:T(8,128)} %get-tuple-element.8), calls=%async_computation.1 | async-start | bytes 1048576 | tf_op jit(solution)/shard_map/all_to_all | solution.py:563
  56.9 0.0 copy-start.3
  56.9 0.0 copy-start.6
  56.9 0.0 copy-start.9
  56.9 12.0 %all_gather.11.refs_13_ = bf16[4,384,256]{2,1,0:T(8,128)(2,1)S(1)} all-gather(bf16[1,384,256]{2,1,0:T(8,128)(2,1)S(1)} %bitcast.15), channel_id=1, replica_groups=mesh['band'=4,'pw'=64] {'band'}, dimensions={0}, use_global_device_ids=true | all-gather | bytes 983040 | tf_op jit(solution)/shard_map/all_gather | solution.py:565
  68.9 6.1 %all-to-all-done.1.refs_1_ = f32[64,16,128]{2,1,0:T(8,128)S(1)} async-done(((f32[64,16,128]{2,1,0:T(8,128)}), f32[64,16,128]{2,1,0:T(8,128)S(1)}, u32[]{:S(2)}, u32[]{:S(2)}) %all-to-all-start.1) | async-done | bytes 524320 | tf_op jit(solution)/shard_map/all_to_all | solution.py:563
  75.0 12.6 %shard_map.160 = bf16[64,16,128]{2,1,0:T(8,128)(2,1)S(1)} custom-call(s32[128,128]{1,0:T(8,128)S(1)} %bitcast.19, f32[64,16,128]{2,1,0:T(8,128)S(1)} %all-to-all-done.1.refs_1_, f32[16,256]{1,0:T(8,128)S(1)} %get-tuple-element.9.refs_2_, bf16[864,256]{1,0:T(8,128)(2,1)S(1)} %get-tuple-element.10.refs_3_, f32[3,192,192]{2,1,0:T(8,128)S(1)} %copy-done.3, ...), custom_call_target="tpu_custom_call" | custom-call | tf_op jit(solution)/shard_map/pallas_call | solution.py:518
  87.6 0.0 copy-start.4
  87.6 20.8 %all_to_all.16.refs_2_ = bf16[64,16,128]{2,1,0:T(8,128)(2,1)S(1)} all-to-all(bf16[64,16,128]{2,1,0:T(8,128)(2,1)S(1)} %shard_map.160), channel_id=1, replica_groups=mesh['band'=4,'pw'=64] {'pw'}, dimensions={0} | all-to-all | bytes 524288 | tf_op jit(solution)/shard_map/all_to_all | solution.py:574
  108.4 1.0 shard_map.161
  (14 shorter events, 0.0 us)
Async XLA Ops:
  7.2 67.8 %all-gather.3.cloned.1.call-start = ((), (), s32[]{:S(2)}) async-start(), calls=%async_computation.3 | async-start | bytes 1310720 | tf_op jit(solution)/shard_map/all_gather | solution.py:564
  7.2 30.8 %copy-start.7 = (bf16[256,512]{1,0:T(8,128)(2,1)S(1)}, bf16[256,512]{1,0:T(8,128)(2,1)}, u32[]{:S(2)}) copy-start(bf16[256,512]{1,0:T(8,128)(2,1)} %constant.18.clone.refs_2_) | copy-start | bytes 786436
  9.4 28.6 %copy-start.2 = (s32[16384]{0:T(1024)S(1)}, s32[16384]{0:T(1024)}, u32[]{:S(2)}) copy-start(s32[16384]{0:T(1024)} %param.16) | copy-start | bytes 196612
  9.4 28.6 %copy-start.5 = (bf16[384,320]{1,0:T(8,128)(2,1)S(1)}, bf16[384,320]{1,0:T(8,128)(2,1)}, u32[]{:S(2)}) copy-start(bf16[384,320]{1,0:T(8,128)(2,1)} %constant.20.clone.refs_4_) | copy-start | bytes 737284
  9.4 28.6 %copy-start.10 = (bf16[64,512]{1,0:T(8,128)(2,1)S(1)}, bf16[64,512]{1,0:T(8,128)(2,1)}, u32[]{:S(2)}) copy-start(bf16[64,512]{1,0:T(8,128)(2,1)} %constant.19.clone.refs_3_) | copy-start | bytes 196612
  38.0 1.0 copy-start
  38.0 0.9 copy-start.12
  38.0 0.9 copy-start.11
  51.0 5.9 %copy-start.1 = (bf16[1,2,192,256]{3,2,1,0:T(8,128)(2,1)S(1)}, bf16[1,2,192,256]{3,2,1,0:T(8,128)(2,1)}, u32[]{:S(2)}) copy-start(bf16[1,2,192,256]{3,2,1,0:T(8,128)(2,1)} %param.15) | copy-start | bytes 589828
  51.0 24.0 %copy-start.8 = (bf16[320,384]{1,0:T(8,128)(2,1)S(1)}, bf16[320,384]{1,0:T(8,128)(2,1)}, u32[]{:S(2)}) copy-start(bf16[320,384]{1,0:T(8,128)(2,1)} %constant.21.clone.refs_9_) | copy-start | bytes 737284
  51.0 23.9 %all-to-all-start.1 = ((f32[64,16,128]{2,1,0:T(8,128)}), f32[64,16,128]{2,1,0:T(8,128)S(1)}, u32[]{:S(2)}, u32[]{:S(2)}) async-start(f32[64,16,128]{2,1,0:T(8,128)} %get-tuple-element.8), calls=%async_computation.1 | async-start | bytes 1048576 | tf_op jit(solution)/shard_map/all_to_all | solution.py:563
  56.9 18.1 %copy-start.3 = (f32[3,192,192]{2,1,0:T(8,128)S(1)}, f32[3,192,192]{2,1,0:T(8,128)}, u32[]{:S(2)}) copy-start(f32[3,192,192]{2,1,0:T(8,128)} %refs_4_.2) | copy-start | bytes 1327108
  56.9 18.1 %copy-start.6 = (bf16[2,256,256]{2,1,0:T(8,128)(2,1)S(1)}, bf16[2,256,256]{2,1,0:T(8,128)(2,1)}, u32[]{:S(2)}) copy-start(bf16[2,256,256]{2,1,0:T(8,128)(2,1)} %constant.22.clone.refs_10_) | copy-start | bytes 786436
  56.9 18.1 %copy-start.9 = (bf16[2,64,256]{2,1,0:T(8,128)(2,1)S(1)}, bf16[2,64,256]{2,1,0:T(8,128)(2,1)}, u32[]{:S(2)}) copy-start(bf16[2,64,256]{2,1,0:T(8,128)(2,1)} %constant.23.clone.refs_11_) | copy-start | bytes 196612
  87.6 20.8 %copy-start.4 = (bf16[384,512]{1,0:T(8,128)(2,1)S(1)}, bf16[384,512]{1,0:T(8,128)(2,1)}, u32[]{:S(2)}) copy-start(bf16[384,512]{1,0:T(8,128)(2,1)} %constant.17.clone.refs_3_) | copy-start | bytes 1179652
Sparse Core Ops, SparseCore 0:
  38.1 17.3 all-gather.2

commit v4 on v3

--- a/solution.py
+++ b/solution.py
@@ -312,12 +312,15 @@
         ).astype(bf16)
         pf_ref[...] = proj()[...].astype(f32)
         ent_weight = dot(slot_onehot(at(), p), weight, ((1,), (1,)))
-        terms = [jnp.zeros((entries, BLOCK), f32) for _ in range(2)]
+        ent_weight = ent_weight.astype(bf16)
+        spread_row = iota((cj, 2 * BLOCK), 0)
+        spread_part = jnp.where(iota((cj, 2 * BLOCK), 1) >= BLOCK, nproj, 0)
+        terms = jnp.zeros((entries, 2 * BLOCK), f32)
         for j in range(nproj):
             values = pf_ref[pl.ds(j, entries, stride=nproj), :]
-            for c in range(2):
-                terms[c] = terms[c] + ent_weight[:, c * nproj + j : c * nproj + j + 1] * values
-        pieces = jnp.concatenate(split3(jnp.concatenate(terms, 1)), 1)
+            wide = dot(ent_weight, ones_where(spread_row == spread_part + j))
+            terms = terms + wide * jnp.concatenate([values, values], 1)
+        pieces = jnp.concatenate(split3(terms), 1)
         rows = block_rows(bi()[...])
         block_row = iota((blocks, LANES), 0)
         hot = jnp.concatenate(

time: 117 us -> 116 us (level)
  no operation moved by 1% of the time
where the time goes in v4:
time: 116 us; the launch traced here: 115 us
  blocking collectives  61.2 us (53%)
  Pallas kernels  27.1 us (23%)
  between operations  14.2 us (12%)
  waiting for transfers between devices  6.08 us (5%)
  starting transfers between devices  5.91 us (5%)
    all_to_all x1, blocking collectives, per_device(): planes = lax.all_to_all(sent, 'pw', split_axis=0, concat_axis=0, tiled=True)  28.5 us
    pallas_call x4, Pallas kernels, call(): pl.pallas_call(body, out_shape=out_shape, in_specs=[hbm if at in late els...  27.1 us
    all_to_all x1, blocking collectives, per_device(): lax.all_to_all(back, 'pw', split_axis=0, concat_axis=0, tiled=True)  20.7 us
    all_gather x1, blocking collectives, per_device(): all_orb = lax.all_gather(orb, 'band', axis=0, tiled=False)  12 us
    all_to_all x1, waiting for transfers between devices, per_device(): lax.all_to_all(to_send, 'pw', split_axis=0, concat_axis=0, tiled=True)  6.06 us
    all_to_all x1, starting transfers between devices, per_device(): lax.all_to_all(to_send, 'pw', split_axis=0, concat_axis=0, tiled=True)  5.87 us
  transfers between devices with their start and end apart: 2, of which 1 were waited for; matrix products, arithmetic and copies ran while one was open for 0% of the time, Pallas kernels for 10%

profile of v4, /device:TPU:6, one launch (start us, length us, event | category | flops | bytes accessed | tf_op | source)
XLA Modules:
  0.0 115.5 jit_solution(9565812489426401008)
XLA Ops:
  7.2 0.0 all-gather.3.cloned.1.call-start
  7.2 0.0 copy-start.7
  7.2 2.2 %shard_map.158 = bf16[64,16,128]{2,1,0:T(8,128)(2,1)} custom-call(s32[128,128]{1,0:T(8,128)} %bitcast.17, bf16[384,256]{1,0:T(8,128)(2,1)} %bitcast.14, bf16[512,384]{1,0:T(8,128)(2,1)} %constant.16.clone.refs_2_), custom_call_target="tpu_custom_call" | custom-call | tf_op jit(solution)/shard_map/pallas_call | solution.py:521
  9.4 0.0 copy-start.2
  9.4 0.0 copy-start.5
  9.4 0.0 copy-start.10
  9.4 28.5 %all_to_all.15.refs_1_ = bf16[64,16,128]{2,1,0:T(8,128)(2,1)} all-to-all(bf16[64,16,128]{2,1,0:T(8,128)(2,1)} %shard_map.158), channel_id=1, replica_groups=mesh['band'=4,'pw'=64] {'pw'}, dimensions={0} | all-to-all | bytes 524288 | tf_op jit(solution)/shard_map/all_to_all | solution.py:555
  38.0 0.0 all-gather.3.cloned.1.call-update
  38.0 0.0 copy-start.12
  38.0 0.0 copy-start.11
  38.1 0.9 copy-done
  39.0 12.0 %shard_map.159 = (bf16[864,256]{1,0:T(8,128)(2,1)S(1)}, f32[16,256]{1,0:T(8,128)S(1)}, f32[64,16,128]{2,1,0:T(8,128)}, f32[64,256]{1,0:T(8,128)S(1)}) custom-call(s32[128,128]{1,0:T(8,128)S(1)} %bitcast.18, bf16[64,16,128]{2,1,0:T(8,128)(2,1)S(1)} %copy-done, bf16[256,512]{1,0:T(8,128)(2,1)S(1)} %copy-done.7, bf16[64,512]{1,0:T(8,128)(2,1)S(1)} %copy-done.10, ...), custom_call_target="tpu_custom_call" | custom-call | tf_op jit(solution)/shard_map/pallas_call | solution.py:521
  51.0 0.0 copy-start.1
  51.0 0.0 copy-start.8
  51.0 5.9 %all-to-all-start.1 = ((f32[64,16,128]{2,1,0:T(8,128)}), f32[64,16,128]{2,1,0:T(8,128)S(1)}, u32[]{:S(2)}, u32[]{:S(2)}) async-start(f32[64,16,128]{2,1,0:T(8,128)} %get-tuple-element.8), calls=%async_computation.1 | async-start | bytes 1048576 | tf_op jit(solution)/shard_map/all_to_all | solution.py:566
  56.9 0.0 copy-start.3
  56.9 0.0 copy-start.6
  56.9 0.0 copy-start.9
  56.9 12.0 %all_gather.11.refs_13_ = bf16[4,384,256]{2,1,0:T(8,128)(2,1)S(1)} all-gather(bf16[1,384,256]{2,1,0:T(8,128)(2,1)S(1)} %bitcast.15), channel_id=1, replica_groups=mesh['band'=4,'pw'=64] {'band'}, dimensions={0}, use_global_device_ids=true | all-gather | bytes 983040 | tf_op jit(solution)/shard_map/all_gather | solution.py:568
  68.9 6.1 %all-to-all-done.1.refs_1_ = f32[64,16,128]{2,1,0:T(8,128)S(1)} async-done(((f32[64,16,128]{2,1,0:T(8,128)}), f32[64,16,128]{2,1,0:T(8,128)S(1)}, u32[]{:S(2)}, u32[]{:S(2)}) %all-to-all-start.1) | async-done | bytes 524320 | tf_op jit(solution)/shard_map/all_to_all | solution.py:566
  75.0 11.9 %shard_map.160 = bf16[64,16,128]{2,1,0:T(8,128)(2,1)S(1)} custom-call(s32[128,128]{1,0:T(8,128)S(1)} %bitcast.19, f32[64,16,128]{2,1,0:T(8,128)S(1)} %all-to-all-done.1.refs_1_, f32[16,256]{1,0:T(8,128)S(1)} %get-tuple-element.9.refs_2_, bf16[864,256]{1,0:T(8,128)(2,1)S(1)} %get-tuple-element.10.refs_3_, f32[3,192,192]{2,1,0:T(8,128)S(1)} %copy-done.3, ...), custom_call_target="tpu_custom_call" | custom-call | tf_op jit(solution)/shard_map/pallas_call | solution.py:521
  86.9 0.0 copy-start.4
  86.9 20.7 %all_to_all.16.refs_2_ = bf16[64,16,128]{2,1,0:T(8,128)(2,1)S(1)} all-to-all(bf16[64,16,128]{2,1,0:T(8,128)(2,1)S(1)} %shard_map.160), channel_id=1, replica_groups=mesh['band'=4,'pw'=64] {'pw'}, dimensions={0} | all-to-all | bytes 524288 | tf_op jit(solution)/shard_map/all_to_all | solution.py:577
  107.6 1.0 shard_map.161
  (14 shorter events, 0.0 us)
Async XLA Ops:
  7.2 67.8 %all-gather.3.cloned.1.call-start = ((), (), s32[]{:S(2)}) async-start(), calls=%async_computation.3 | async-start | bytes 1310720 | tf_op jit(solution)/shard_map/all_gather | solution.py:567
  7.2 30.8 %copy-start.7 = (bf16[256,512]{1,0:T(8,128)(2,1)S(1)}, bf16[256,512]{1,0:T(8,128)(2,1)}, u32[]{:S(2)}) copy-start(bf16[256,512]{1,0:T(8,128)(2,1)} %constant.18.clone.refs_2_) | copy-start | bytes 786436
  9.4 28.6 %copy-start.2 = (s32[16384]{0:T(1024)S(1)}, s32[16384]{0:T(1024)}, u32[]{:S(2)}) copy-start(s32[16384]{0:T(1024)} %param.16) | copy-start | bytes 196612
  9.4 28.6 %copy-start.5 = (bf16[384,320]{1,0:T(8,128)(2,1)S(1)}, bf16[384,320]{1,0:T(8,128)(2,1)}, u32[]{:S(2)}) copy-start(bf16[384,320]{1,0:T(8,128)(2,1)} %constant.20.clone.refs_4_) | copy-start | bytes 737284
  9.4 28.6 %copy-start.10 = (bf16[64,512]{1,0:T(8,128)(2,1)S(1)}, bf16[64,512]{1,0:T(8,128)(2,1)}, u32[]{:S(2)}) copy-start(bf16[64,512]{1,0:T(8,128)(2,1)} %constant.19.clone.refs_3_) | copy-start | bytes 196612
  38.0 1.0 copy-start
  38.0 0.9 copy-start.12
  38.0 0.9 copy-start.11
  51.0 5.9 %copy-start.1 = (bf16[1,2,192,256]{3,2,1,0:T(8,128)(2,1)S(1)}, bf16[1,2,192,256]{3,2,1,0:T(8,128)(2,1)}, u32[]{:S(2)}) copy-start(bf16[1,2,192,256]{3,2,1,0:T(8,128)(2,1)} %param.15) | copy-start | bytes 589828
  51.0 24.0 %copy-start.8 = (bf16[320,384]{1,0:T(8,128)(2,1)S(1)}, bf16[320,384]{1,0:T(8,128)(2,1)}, u32[]{:S(2)}) copy-start(bf16[320,384]{1,0:T(8,128)(2,1)} %constant.21.clone.refs_9_) | copy-start | bytes 737284
  51.0 23.9 %all-to-all-start.1 = ((f32[64,16,128]{2,1,0:T(8,128)}), f32[64,16,128]{2,1,0:T(8,128)S(1)}, u32[]{:S(2)}, u32[]{:S(2)}) async-start(f32[64,16,128]{2,1,0:T(8,128)} %get-tuple-element.8), calls=%async_computation.1 | async-start | bytes 1048576 | tf_op jit(solution)/shard_map/all_to_all | solution.py:566
  56.9 18.1 %copy-start.3 = (f32[3,192,192]{2,1,0:T(8,128)S(1)}, f32[3,192,192]{2,1,0:T(8,128)}, u32[]{:S(2)}) copy-start(f32[3,192,192]{2,1,0:T(8,128)} %refs_4_.2) | copy-start | bytes 1327108
  56.9 18.1 %copy-start.6 = (bf16[2,256,256]{2,1,0:T(8,128)(2,1)S(1)}, bf16[2,256,256]{2,1,0:T(8,128)(2,1)}, u32[]{:S(2)}) copy-start(bf16[2,256,256]{2,1,0:T(8,128)(2,1)} %constant.22.clone.refs_10_) | copy-start | bytes 786436
  56.9 18.1 %copy-start.9 = (bf16[2,64,256]{2,1,0:T(8,128)(2,1)S(1)}, bf16[2,64,256]{2,1,0:T(8,128)(2,1)}, u32[]{:S(2)}) copy-start(bf16[2,64,256]{2,1,0:T(8,128)(2,1)} %constant.23.clone.refs_11_) | copy-start | bytes 196612
  86.9 20.8 %copy-start.4 = (bf16[384,512]{1,0:T(8,128)(2,1)S(1)}, bf16[384,512]{1,0:T(8,128)(2,1)}, u32[]{:S(2)}) copy-start(bf16[384,512]{1,0:T(8,128)(2,1)} %constant.17.clone.refs_3_) | copy-start | bytes 1179652
Sparse Core Ops, SparseCore 0:
  38.1 17.3 all-gather.2

commit v5 on v4

--- a/solution.py
+++ b/solution.py
@@ -268,15 +268,14 @@
         picked = dot(hot, rs_ref[...])
         select_row = iota((2 * BLOCK, LANES), 0)
         select_lane = iota((2 * BLOCK, LANES), 1)
-        corr = jnp.zeros((entries, LANES), f32)
+        products, selects = [], []
         for j in range(nproj):
             values = pf_ref[pl.ds(j, entries, stride=nproj), :]
             product = jnp.concatenate([values, values], 1) * picked
             hi = product.astype(bf16)
-            low = (product - hi.astype(f32)).astype(bf16)
-            target = jnp.where(select_row >= BLOCK, nproj + j, j)
-            ones = ones_where(select_lane == target)
-            corr = corr + (dot(hi, ones) + dot(low, ones))
+            products += [hi, (product - hi.astype(f32)).astype(bf16)]
+            selects += [ones_where(select_lane == jnp.where(select_row >= BLOCK, nproj + j, j))] * 2
+        corr = dot(jnp.concatenate(products, 1), jnp.concatenate(selects, 0))
         pieces = jnp.concatenate(split3(corr), 1)
         window = dot(pieces, slot_onehot(at(), p), ((0,), (0,)))
         window = window[0:cj] + window[LANES : LANES + cj] + window[2 * LANES : 2 * LANES + cj]

time: 116 us -> 116 us (level)
  no operation moved by 1% of the time
where the time goes in v5:
time: 116 us; the launch traced here: 115 us
  blocking collectives  61.2 us (53%)
  Pallas kernels  27.1 us (23%)
  between operations  14.2 us (12%)
  waiting for transfers between devices  6.08 us (5%)
  starting transfers between devices  5.91 us (5%)
    all_to_all x1, blocking collectives, per_device(): planes = lax.all_to_all(sent, 'pw', split_axis=0, concat_axis=0, tiled=True)  28.5 us
    pallas_call x4, Pallas kernels, call(): pl.pallas_call(body, out_shape=out_shape, in_specs=[hbm if at in late els...  27.1 us
    all_to_all x1, blocking collectives, per_device(): lax.all_to_all(back, 'pw', split_axis=0, concat_axis=0, tiled=True)  20.7 us
    all_gather x1, blocking collectives, per_device(): all_orb = lax.all_gather(orb, 'band', axis=0, tiled=False)  12 us
    all_to_all x1, waiting for transfers between devices, per_device(): lax.all_to_all(to_send, 'pw', split_axis=0, concat_axis=0, tiled=True)  6.06 us
    all_to_all x1, starting transfers between devices, per_device(): lax.all_to_all(to_send, 'pw', split_axis=0, concat_axis=0, tiled=True)  5.87 us
  transfers between devices with their start and end apart: 2, of which 1 were waited for; matrix products, arithmetic and copies ran while one was open for 0% of the time, Pallas kernels for 10%

profile of v5, /device:TPU:6, one launch (start us, length us, event | category | flops | bytes accessed | tf_op | source)
XLA Modules:
  0.0 115.5 jit_solution(14754255711371451549)
XLA Ops:
  7.2 0.0 all-gather.3.cloned.1.call-start
  7.2 0.0 copy-start.7
  7.2 2.2 %shard_map.158 = bf16[64,16,128]{2,1,0:T(8,128)(2,1)} custom-call(s32[128,128]{1,0:T(8,128)} %bitcast.17, bf16[384,256]{1,0:T(8,128)(2,1)} %bitcast.14, bf16[512,384]{1,0:T(8,128)(2,1)} %constant.16.clone.refs_2_), custom_call_target="tpu_custom_call" | custom-call | tf_op jit(solution)/shard_map/pallas_call | solution.py:520
  9.4 0.0 copy-start.2
  9.4 0.0 copy-start.5
  9.4 0.0 copy-start.10
  9.4 28.5 %all_to_all.15.refs_1_ = bf16[64,16,128]{2,1,0:T(8,128)(2,1)} all-to-all(bf16[64,16,128]{2,1,0:T(8,128)(2,1)} %shard_map.158), channel_id=1, replica_groups=mesh['band'=4,'pw'=64] {'pw'}, dimensions={0} | all-to-all | bytes 524288 | tf_op jit(solution)/shard_map/all_to_all | solution.py:554
  38.0 0.0 all-gather.3.cloned.1.call-update
  38.0 0.0 copy-start.12
  38.0 0.0 copy-start.11
  38.1 0.9 copy-done
  39.0 12.0 %shard_map.159 = (bf16[864,256]{1,0:T(8,128)(2,1)S(1)}, f32[16,256]{1,0:T(8,128)S(1)}, f32[64,16,128]{2,1,0:T(8,128)}, f32[64,256]{1,0:T(8,128)S(1)}) custom-call(s32[128,128]{1,0:T(8,128)S(1)} %bitcast.18, bf16[64,16,128]{2,1,0:T(8,128)(2,1)S(1)} %copy-done, bf16[256,512]{1,0:T(8,128)(2,1)S(1)} %copy-done.7, bf16[64,512]{1,0:T(8,128)(2,1)S(1)} %copy-done.10, ...), custom_call_target="tpu_custom_call" | custom-call | tf_op jit(solution)/shard_map/pallas_call | solution.py:520
  51.0 0.0 copy-start.1
  51.0 0.0 copy-start.8
  51.0 5.9 %all-to-all-start.1 = ((f32[64,16,128]{2,1,0:T(8,128)}), f32[64,16,128]{2,1,0:T(8,128)S(1)}, u32[]{:S(2)}, u32[]{:S(2)}) async-start(f32[64,16,128]{2,1,0:T(8,128)} %get-tuple-element.8), calls=%async_computation.1 | async-start | bytes 1048576 | tf_op jit(solution)/shard_map/all_to_all | solution.py:565
  56.9 0.0 copy-start.3
  56.9 0.0 copy-start.6
  56.9 0.0 copy-start.9
  56.9 12.0 %all_gather.11.refs_13_ = bf16[4,384,256]{2,1,0:T(8,128)(2,1)S(1)} all-gather(bf16[1,384,256]{2,1,0:T(8,128)(2,1)S(1)} %bitcast.15), channel_id=1, replica_groups=mesh['band'=4,'pw'=64] {'band'}, dimensions={0}, use_global_device_ids=true | all-gather | bytes 983040 | tf_op jit(solution)/shard_map/all_gather | solution.py:567
  68.9 6.1 %all-to-all-done.1.refs_1_ = f32[64,16,128]{2,1,0:T(8,128)S(1)} async-done(((f32[64,16,128]{2,1,0:T(8,128)}), f32[64,16,128]{2,1,0:T(8,128)S(1)}, u32[]{:S(2)}, u32[]{:S(2)}) %all-to-all-start.1) | async-done | bytes 524320 | tf_op jit(solution)/shard_map/all_to_all | solution.py:565
  75.0 11.9 %shard_map.160 = bf16[64,16,128]{2,1,0:T(8,128)(2,1)S(1)} custom-call(s32[128,128]{1,0:T(8,128)S(1)} %bitcast.19, f32[64,16,128]{2,1,0:T(8,128)S(1)} %all-to-all-done.1.refs_1_, f32[16,256]{1,0:T(8,128)S(1)} %get-tuple-element.9.refs_2_, bf16[864,256]{1,0:T(8,128)(2,1)S(1)} %get-tuple-element.10.refs_3_, f32[3,192,192]{2,1,0:T(8,128)S(1)} %copy-done.3, ...), custom_call_target="tpu_custom_call" | custom-call | tf_op jit(solution)/shard_map/pallas_call | solution.py:520
  86.8 0.0 copy-start.4
  86.8 20.7 %all_to_all.16.refs_2_ = bf16[64,16,128]{2,1,0:T(8,128)(2,1)S(1)} all-to-all(bf16[64,16,128]{2,1,0:T(8,128)(2,1)S(1)} %shard_map.160), channel_id=1, replica_groups=mesh['band'=4,'pw'=64] {'pw'}, dimensions={0} | all-to-all | bytes 524288 | tf_op jit(solution)/shard_map/all_to_all | solution.py:576
  107.6 1.0 shard_map.161
  (14 shorter events, 0.0 us)
Async XLA Ops:
  7.2 67.8 %all-gather.3.cloned.1.call-start = ((), (), s32[]{:S(2)}) async-start(), calls=%async_computation.3 | async-start | bytes 1310720 | tf_op jit(solution)/shard_map/all_gather | solution.py:566
  7.2 30.8 %copy-start.7 = (bf16[256,512]{1,0:T(8,128)(2,1)S(1)}, bf16[256,512]{1,0:T(8,128)(2,1)}, u32[]{:S(2)}) copy-start(bf16[256,512]{1,0:T(8,128)(2,1)} %constant.18.clone.refs_2_) | copy-start | bytes 786436
  9.4 28.6 %copy-start.2 = (s32[16384]{0:T(1024)S(1)}, s32[16384]{0:T(1024)}, u32[]{:S(2)}) copy-start(s32[16384]{0:T(1024)} %param.16) | copy-start | bytes 196612
  9.4 28.6 %copy-start.5 = (bf16[384,320]{1,0:T(8,128)(2,1)S(1)}, bf16[384,320]{1,0:T(8,128)(2,1)}, u32[]{:S(2)}) copy-start(bf16[384,320]{1,0:T(8,128)(2,1)} %constant.20.clone.refs_4_) | copy-start | bytes 737284
  9.4 28.6 %copy-start.10 = (bf16[64,512]{1,0:T(8,128)(2,1)S(1)}, bf16[64,512]{1,0:T(8,128)(2,1)}, u32[]{:S(2)}) copy-start(bf16[64,512]{1,0:T(8,128)(2,1)} %constant.19.clone.refs_3_) | copy-start | bytes 196612
  38.0 1.0 copy-start
  38.0 0.9 copy-start.12
  38.0 0.9 copy-start.11
  51.0 5.9 %copy-start.1 = (bf16[1,2,192,256]{3,2,1,0:T(8,128)(2,1)S(1)}, bf16[1,2,192,256]{3,2,1,0:T(8,128)(2,1)}, u32[]{:S(2)}) copy-start(bf16[1,2,192,256]{3,2,1,0:T(8,128)(2,1)} %param.15) | copy-start | bytes 589828
  51.0 24.0 %copy-start.8 = (bf16[320,384]{1,0:T(8,128)(2,1)S(1)}, bf16[320,384]{1,0:T(8,128)(2,1)}, u32[]{:S(2)}) copy-start(bf16[320,384]{1,0:T(8,128)(2,1)} %constant.21.clone.refs_9_) | copy-start | bytes 737284
  51.0 23.9 %all-to-all-start.1 = ((f32[64,16,128]{2,1,0:T(8,128)}), f32[64,16,128]{2,1,0:T(8,128)S(1)}, u32[]{:S(2)}, u32[]{:S(2)}) async-start(f32[64,16,128]{2,1,0:T(8,128)} %get-tuple-element.8), calls=%async_computation.1 | async-start | bytes 1048576 | tf_op jit(solution)/shard_map/all_to_all | solution.py:565
  56.9 18.1 %copy-start.3 = (f32[3,192,192]{2,1,0:T(8,128)S(1)}, f32[3,192,192]{2,1,0:T(8,128)}, u32[]{:S(2)}) copy-start(f32[3,192,192]{2,1,0:T(8,128)} %refs_4_.2) | copy-start | bytes 1327108
  56.9 18.1 %copy-start.6 = (bf16[2,256,256]{2,1,0:T(8,128)(2,1)S(1)}, bf16[2,256,256]{2,1,0:T(8,128)(2,1)}, u32[]{:S(2)}) copy-start(bf16[2,256,256]{2,1,0:T(8,128)(2,1)} %constant.22.clone.refs_10_) | copy-start | bytes 786436
  56.9 18.1 %copy-start.9 = (bf16[2,64,256]{2,1,0:T(8,128)(2,1)S(1)}, bf16[2,64,256]{2,1,0:T(8,128)(2,1)}, u32[]{:S(2)}) copy-start(bf16[2,64,256]{2,1,0:T(8,128)(2,1)} %constant.23.clone.refs_11_) | copy-start | bytes 196612
  86.8 20.8 %copy-start.4 = (bf16[384,512]{1,0:T(8,128)(2,1)S(1)}, bf16[384,512]{1,0:T(8,128)(2,1)}, u32[]{:S(2)}) copy-start(bf16[384,512]{1,0:T(8,128)(2,1)} %constant.17.clone.refs_3_) | copy-start | bytes 1179652
Sparse Core Ops, SparseCore 0:
  38.1 17.3 all-gather.2
